TPU v7x, 256 devices: a whole 4x4x8 slice. The times are simulated.
256 devices in a mesh: expert: 64 (over z, x, core), tensor: 4 (over y).
Axes of the slice: x: 4, y: 4, z: 8, core: 2. Of those that a mesh axis runs over, the one named last changes fastest.
Arguments:
- tokens: bfloat16 [2048, 7168], P('expert'), may hold values from -6 to 6
- routes: int32 [2048, 8], P('expert'), may hold values from 0 to 63, all different within a row; in each aligned block of 32 rows (0 to 31, 32 to 63, ...) at most 8 rows name the same one
- gate_weight: bfloat16 [64, 7168, 1024], P('expert', None, 'tensor'), may hold values from -0.0625 to 0.0625
- up_weight: bfloat16 [64, 7168, 1024], P('expert', None, 'tensor'), may hold values from -0.0625 to 0.0625
- down_weight: bfloat16 [64, 1024, 3584], P('expert', 'tensor'), may hold values from -6 to 6
- removed: int32 [64, 256], P('expert'), may hold values from 0 to 1023, as said below
Outputs:
- pruned_down: bfloat16 [64, 1024, 3584], P('expert', 'tensor')
Inputs may be any that keep to these rules, and one draw needn't show every extreme that they name: `routes`: among the rows of one index of expert no expert is named more than 8 times, a bound that some block reaches. `removed`: each row holds 256 different hidden units.
All inputs are finite; a program needn't handle non-finite values.
Results may differ from a plain program's by a relative error of at most 0.005.
Values may be sent and summed in bfloat16 or wider, within the bound.
A program may use at most 128 MiB of HBM per device.

v0:
```python
import jax
import jax.numpy as jnp
from jax import lax
from jax.sharding import PartitionSpec as P

DAMPING = 0.1


def placing_matrix(routes, experts, capacity):
    tok_rows, top = routes.shape
    flat = routes.reshape(-1)
    onehot = (flat[:, None] == jnp.arange(experts, dtype=jnp.int32)[None, :]).astype(jnp.int32)
    before = jnp.cumsum(onehot, axis=0) - onehot
    slot_in = jnp.sum(before * onehot, axis=1)
    target = (flat * capacity + slot_in).reshape(tok_rows, top)
    slots = jnp.arange(experts * capacity, dtype=jnp.int32)
    hits = target[None, :, :] == slots[:, None, None]
    return jnp.sum(hits.astype(jnp.float32), axis=2).astype(jnp.bfloat16)


def local(tokens, routes, gate_weight, up_weight, down_weight, removed):
    groups = lax.axis_size("expert")
    experts = groups * gate_weight.shape[0]
    tok_rows, width = tokens.shape
    top = routes.shape[1]
    capacity = min(tok_rows, max(2, 2 * tok_rows * top // experts))
    placing = placing_matrix(routes, experts, capacity)
    outgoing = jnp.dot(placing, tokens, preferred_element_type=jnp.float32).astype(jnp.bfloat16)
    outgoing = outgoing.reshape(experts, capacity, width)
    arrived = lax.all_to_all(outgoing, "expert", split_axis=0, concat_axis=0, tiled=True)
    rows = arrived.reshape(experts * capacity, width)
    gate = jnp.dot(rows, gate_weight[0], preferred_element_type=jnp.float32)
    up = jnp.dot(rows, up_weight[0], preferred_element_type=jnp.float32)
    hidden = (jax.nn.silu(gate) * up).astype(jnp.bfloat16)
    every = lax.all_gather(hidden, "tensor", axis=1, tiled=True)
    contract = (((0,), (0,)), ((), ()))
    gram = lax.dot_general(every, every, contract, preferred_element_type=jnp.float32)
    order = gram.shape[0]
    shift = DAMPING * jnp.mean(jnp.diagonal(gram)) + 1e-06
    damped = gram + shift * jnp.eye(order, dtype=jnp.float32)
    lower = jnp.linalg.cholesky(damped)
    chosen = removed[0]
    picks = (jnp.arange(order, dtype=jnp.int32)[:, None] == chosen[None, :]).astype(jnp.float32)
    columns = jax.scipy.linalg.cho_solve((lower, True), picks)
    block = jnp.take(columns, chosen, axis=0)
    block = 0.5 * (block + block.T)
    inner = jnp.linalg.cholesky(block)
    mixing = jax.scipy.linalg.cho_solve((inner, True), columns.T).T
    own_rows = down_weight.shape[1]
    first = lax.axis_index("tensor") * own_rows
    own_mix = lax.dynamic_slice_in_dim(mixing, first, own_rows, 0)
    own_picks = lax.dynamic_slice_in_dim(picks, first, own_rows, 0)
    term = jnp.dot(
        own_picks.T.astype(jnp.bfloat16), down_weight[0], preferred_element_type=jnp.float32
    )
    dropped = lax.psum(term.astype(jnp.bfloat16), "tensor").astype(jnp.float32)
    fixed_rows = down_weight[0].astype(jnp.float32) - jnp.dot(
        own_mix, dropped, precision=lax.Precision.HIGHEST
    )
    keep = 1.0 - jnp.sum(own_picks, axis=1, keepdims=True)
    return (fixed_rows * keep).astype(jnp.bfloat16)[None]


def solution(mesh):
    in_specs = (
        P("expert", None),
        P("expert", None),
        P("expert", None, "tensor"),
        P("expert", None, "tensor"),
        P("expert", "tensor", None),
        P("expert", None),
    )
    out_specs = P("expert", "tensor", None)
    return jax.shard_map(local, mesh=mesh, in_specs=in_specs, out_specs=out_specs, check_vma=False)
```

profile of v0, /device:TPU:1, one launch (start us, length us, event | category | flops | bytes accessed | tf_op | source)
XLA Modules:
  0.0 681.8 jit_solution(1581595775817547163)
XLA Ops:
  11.0 175.7 %all_to_all.5 = bf16[64,8,7168]{2,1,0:T(8,128)(2,1)S(1)} all-to-all(bf16[64,8,7168]{2,1,0:T(8,128)(2,1)S(1)} %fusion), channel_id=1, replica_groups=mesh['expert'=64,'tensor'=4] {'expert'}, dimensions={0} | all-to-all | bytes 14680064 | tf_op jit(solution)/shard_map/all_to_all | solution.py:30
  194.8 22.0 %all-gather.2.cloned.1.call-done = bf16[512,1024]{1,0:T(8,128)(2,1)} async-done(((bf16[512,256]{1,0:T(8,128)(2,1)}), bf16[512,1024]{1,0:T(8,128)(2,1)}) %all-gather.2.cloned.1.call-update) | async-done | bytes 1048592 | tf_op jit(solution)/shard_map/all_gather | solution.py:35
  226.9 17.5 %gather_fusion = f32[1024]{0:T(1024)S(1)} fusion(f32[1024,1024]{1,0:T(8,128)} %fusion.141, s32[1024]{0:T(1024)S(1)} %bitcast.230), kind=kCustom, calls=%fused_computation | custom fusion | bytes 16384 | tf_op jit(solution)/shard_map/jit(diagonal)/cond/branch_0_fun/gather | solution.py:39
  252.1 11.7 %cholesky.248 = f32[128,128]{1,0:T(8,128)S(1)} custom-call(f32[128,128]{1,0:T(8,128)S(1)} %cholesky.647), custom_call_target="Cholesky" | custom-call | tf_op jit(solution)/shard_map/jit(cholesky)/cholesky | solution.py:41
  266.4 9.8 %custom-call.77 = f32[1,128,128]{1,2,0:T(8,128)S(1)} custom-call(f32[1,128,128]{2,1,0:T(8,128)S(1)} %get-tuple-element.94), custom_call_target="InvertDiagBlocksLowerTriangular" | custom-call | tf_op jit(solution)/shard_map/jit(cholesky)/cholesky | solution.py:41
  280.9 12.1 %cholesky.271 = f32[128,128]{1,0:T(8,128)S(1)} custom-call(f32[128,128]{1,0:T(8,128)S(1)} %cholesky.651), custom_call_target="Cholesky" | custom-call | tf_op jit(solution)/shard_map/jit(cholesky)/cholesky | solution.py:41
  293.6 9.8 %custom-call.78 = f32[1,128,128]{1,2,0:T(8,128)S(1)} custom-call(f32[1,128,128]{2,1,0:T(8,128)S(1)} %get-tuple-element.91), custom_call_target="InvertDiagBlocksLowerTriangular" | custom-call | tf_op jit(solution)/shard_map/jit(cholesky)/cholesky | solution.py:41
  307.8 11.7 %cholesky.298 = f32[128,128]{1,0:T(8,128)S(1)} custom-call(f32[128,128]{1,0:T(8,128)S(1)} %cholesky.656), custom_call_target="Cholesky" | custom-call | tf_op jit(solution)/shard_map/jit(cholesky)/cholesky | solution.py:41
  320.8 9.8 %custom-call.79 = f32[1,128,128]{1,2,0:T(8,128)S(1)} custom-call(f32[1,128,128]{2,1,0:T(8,128)S(1)} %get-tuple-element.88), custom_call_target="InvertDiagBlocksLowerTriangular" | custom-call | tf_op jit(solution)/shard_map/jit(cholesky)/cholesky | solution.py:41
  334.2 11.9 %cholesky.537 = f32[128,128]{1,0:T(8,128)S(1)} custom-call(f32[128,128]{1,0:T(8,128)S(1)} %cholesky.661), custom_call_target="Cholesky" | custom-call | tf_op jit(solution)/shard_map/jit(cholesky)/cholesky | solution.py:41
  347.4 9.8 %custom-call.80 = f32[1,128,128]{1,2,0:T(8,128)S(1)} custom-call(f32[1,128,128]{2,1,0:T(8,128)S(1)} %get-tuple-element.85), custom_call_target="InvertDiagBlocksLowerTriangular" | custom-call | tf_op jit(solution)/shard_map/jit(cholesky)/cholesky | solution.py:41
  360.7 11.7 %cholesky.556 = f32[128,128]{1,0:T(8,128)S(1)} custom-call(f32[128,128]{1,0:T(8,128)S(1)} %cholesky.666), custom_call_target="Cholesky" | custom-call | tf_op jit(solution)/shard_map/jit(cholesky)/cholesky | solution.py:41
  373.7 10.0 %custom-call.81 = f32[1,128,128]{1,2,0:T(8,128)S(1)} custom-call(f32[1,128,128]{2,1,0:T(8,128)S(1)} %get-tuple-element.82), custom_call_target="InvertDiagBlocksLowerTriangular" | custom-call | tf_op jit(solution)/shard_map/jit(cholesky)/cholesky | solution.py:41
  387.0 11.7 %cholesky.576 = f32[128,128]{1,0:T(8,128)S(1)} custom-call(f32[128,128]{1,0:T(8,128)S(1)} %cholesky.671), custom_call_target="Cholesky" | custom-call | tf_op jit(solution)/shard_map/jit(cholesky)/cholesky | solution.py:41
  400.0 9.8 %custom-call.82 = f32[1,128,128]{1,2,0:T(8,128)S(1)} custom-call(f32[1,128,128]{2,1,0:T(8,128)S(1)} %get-tuple-element.79), custom_call_target="InvertDiagBlocksLowerTriangular" | custom-call | tf_op jit(solution)/shard_map/jit(cholesky)/cholesky | solution.py:41
  412.8 12.1 %cholesky.596 = f32[128,128]{1,0:T(8,128)S(1)} custom-call(f32[128,128]{1,0:T(8,128)S(1)} %cholesky.676), custom_call_target="Cholesky" | custom-call | tf_op jit(solution)/shard_map/jit(cholesky)/cholesky | solution.py:41
  426.2 9.8 %custom-call.88 = f32[1,128,128]{1,2,0:T(8,128)S(1)} custom-call(f32[1,128,128]{2,1,0:T(8,128)S(1)} %get-tuple-element.76), custom_call_target="InvertDiagBlocksLowerTriangular" | custom-call | tf_op jit(solution)/shard_map/jit(cholesky)/cholesky/custom-call.20 | solution.py:41
  438.6 11.7 %cholesky.610 = f32[128,128]{1,0:T(8,128)S(1)} custom-call(f32[128,128]{1,0:T(8,128)S(1)} %convolution_subtract_fusion.24), custom_call_target="Cholesky" | custom-call | tf_op jit(solution)/shard_map/jit(cholesky)/cholesky | solution.py:41
  462.2 28.6 %while.2 = (s32[]{:T(128)}, f32[1024,1024]{1,0:T(8,128)}, s32[8,2]{0,1:T(2,128)S(1)}, f32[8,128,128]{2,1,0:T(8,128)}, s32[]{:T(128)}) while((s32[]{:T(128)}, f32[1024,1024]{1,0:T(8,128)}, s32[8,2]{0,1:T(2,128)S(1)}, f32[8,128,128]{2,1,0:T(8,128)}, s32[]{:T(128)}) %tuple.77), condition=%wide.while_cond, body=%wide.while_body.sunk | while | flops 2 | bytes 132705 | solution.py:44
  490.9 80.2 %custom-call.83 = f32[8,128,128]{1,2,0:T(8,128)} custom-call(f32[8,128,128]{2,1,0:T(8,128)} %get-tuple-element.13), custom_call_target="InvertDiagBlocksLowerTriangular" | custom-call | tf_op jit(solution)/shard_map/jit(_cho_solve)/triangular_solve | solution.py:44
  597.0 11.9 %cholesky.623 = f32[128,128]{1,0:T(8,128)S(1)} custom-call(f32[128,128]{1,0:T(8,128)S(1)} %cholesky.680), custom_call_target="Cholesky" | custom-call | tf_op jit(solution)/shard_map/jit(cholesky)/cholesky | solution.py:47
  609.8 9.8 %custom-call.89 = f32[1,128,128]{1,2,0:T(8,128)S(1)} custom-call(f32[1,128,128]{2,1,0:T(8,128)S(1)} %get-tuple-element.72), custom_call_target="InvertDiagBlocksLowerTriangular" | custom-call | tf_op jit(solution)/shard_map/jit(cholesky)/cholesky/custom-call.20 | solution.py:47
  622.5 11.7 %cholesky.632 = f32[128,128]{1,0:T(8,128)S(1)} custom-call(f32[128,128]{1,0:T(8,128)S(1)} %convolution_subtract_fusion.23), custom_call_target="Cholesky" | custom-call | tf_op jit(solution)/shard_map/jit(cholesky)/cholesky | solution.py:47
  644.1 20.8 %custom-call.84 = f32[2,128,128]{1,2,0:T(8,128)S(1)} custom-call(f32[2,128,128]{2,1,0:T(8,128)} %get-tuple-element.21), custom_call_target="InvertDiagBlocksLowerTriangular" | custom-call | tf_op jit(solution)/shard_map/jit(_cho_solve)/triangular_solve | solution.py:48
  (211 shorter events, 152.5 us)
Async XLA Ops:
  6.5 2.3 copy-start
  6.5 210.2 %all-gather.2.cloned.1.call-start = ((), (), s32[]{:S(2)}) async-start(), calls=%async_computation.1 | async-start | bytes 1310720 | tf_op jit(solution)/shard_map/all_gather | solution.py:35
  10.9 175.8 %copy-start.10 = (bf16[1,7168,256]{2,1,0:T(8,128)(2,1)S(1)}, bf16[1,7168,256]{2,1,0:T(8,128)(2,1)}, u32[]{:S(2)}) copy-start(bf16[1,7168,256]{2,1,0:T(8,128)(2,1)} %param.10) | copy-start | bytes 11010052
  186.7 2.1 copy-start.11
  188.8 2.9 copy-start.9
  188.8 3.8 copy-start.4
  191.7 478.2 %all-reduce.4.cloned.1.call-start = ((), (), s32[]{:S(2)}) async-start(), calls=%async_computation.2 | async-start | bytes 3670016 | tf_op jit(solution)/shard_map/psum | solution.py:56
  250.2 1.9 copy-start.3
  280.1 0.8 copy-start.7
  571.0 8.6 %copy-start.2 = (f32[1024,1024]{1,0:T(8,128)S(1)}, f32[1024,1024]{1,0:T(8,128)}, u32[]{:S(2)}) copy-start(f32[1024,1024]{1,0:T(8,128)} %get-tuple-element.207) | copy-start | bytes 12582916
  571.1 9.0 %copy-start.5 = (f32[8,128,128]{1,2,0:T(8,128)S(1)}, f32[8,128,128]{1,2,0:T(8,128)}, u32[]{:S(2)}) copy-start(f32[8,128,128]{1,2,0:T(8,128)} %custom-call.83) | copy-start | bytes 1572868
  596.3 0.7 copy-start.8
  644.1 23.1 %copy-start.6 = (f32[256,256]{0,1:T(8,128)}, f32[256,256]{0,1:T(8,128)S(1)}, u32[]{:S(2)}) copy-start(f32[256,256]{0,1:T(8,128)S(1)} %get-tuple-element.211) | copy-start | bytes 786436
  667.8 6.7 copy-start.1
Sparse Core Ops, SparseCore 0:
  191.8 24.9 all-gather.1
  219.1 61.5 all-reduce.3
where the time goes:
time: 691 us; the launch traced here: 682 us
  other arithmetic  323 us (47%)
  blocking collectives  176 us (25%)
  local copies, waits for them, and re-layouts  70.6 us (10%)
  matrix products  68.5 us (10%)
  waiting for transfers between devices  22 us (3%)
  between operations  21.7 us (3%)
    all_to_all x1, blocking collectives, local(): lax.all_to_all(outgoing, 'expert', split_axis=0, concat_axis=0, tiled=True)  176 us
    another operation x30, other arithmetic, local(): lower = jnp.linalg.cholesky(damped)  173 us
    another operation x3, other arithmetic, local(): columns = jax.scipy.linalg.cho_solve((lower, True), picks)  85 us
    another operation x7, other arithmetic, local(): inner = jnp.linalg.cholesky(block)  34.8 us
    another operation x36, local copies, waits for them, and re-layouts  34.3 us
    another operation x14, matrix products, local(): lower = jnp.linalg.cholesky(damped)  24.1 us
    all_gather x1, waiting for transfers between devices, local(): every = lax.all_gather(hidden, 'tensor', axis=1, tiled=True)  22 us
    another operation x3, other arithmetic, local(): mixing = jax.scipy.linalg.cho_solve((inner, True), columns.T).T  21.8 us
  transfers between devices with their start and end apart: 2, of which 1 were waited for; matrix products, arithmetic and copies ran while one was open for 65% of the time, Pallas kernels for 0%

commit v1 on v0

v1 whole, which is shorter than its diff:
```python
import functools

import jax
import jax.numpy as jnp
from jax import lax
from jax.experimental import pallas as pl
from jax.experimental.pallas import tpu as pltpu
from jax.sharding import PartitionSpec as P

DAMPING = 0.1
F32 = jnp.float32
BF16 = jnp.bfloat16
SINGLE = 2
ROUNDS = 9
CAP = 1.85


def placing_matrix(routes, experts, capacity):
    tok_rows, top = routes.shape
    flat = routes.reshape(-1)
    onehot = (flat[:, None] == jnp.arange(experts, dtype=jnp.int32)[None, :]).astype(jnp.int32)
    before = jnp.cumsum(onehot, axis=0) - onehot
    slot_in = jnp.sum(before * onehot, axis=1)
    target = (flat * capacity + slot_in).reshape(tok_rows, top)
    slots = jnp.arange(experts * capacity, dtype=jnp.int32)
    hits = target[None, :, :] == slots[:, None, None]
    return jnp.sum(hits.astype(F32), axis=2).astype(BF16)


def dot(a, b, left=1, right=0):
    return lax.dot_general(a, b, (((left,), (right,)), ((), ())), preferred_element_type=F32)


def split(x):
    high = x.astype(BF16)
    return high, (x - high.astype(F32)).astype(BF16)


def three(ah, al, bh, bl):
    return dot(ah, bh) + dot(ah, bl) + dot(al, bh)


def scales(lowest, rounds):
    out = []
    for _ in range(rounds):
        scale = min(2.0 / (1.0 + lowest), CAP)
        out.append(scale)
        lowest = 1.0 - (1.0 - scale * lowest) ** 2
    return out


def solve_kernel(every_ref, chosen_ref, mix_ref):
    parts, rows, own = every_ref.shape
    count = chosen_ref.shape[1]
    order = parts * own
    chosen = chosen_ref[...]
    total = jnp.zeros((1, 1), F32)
    removed = jnp.zeros((rows, count), F32)
    gram = jnp.zeros((rows, rows), F32)
    for part in range(parts):
        block = every_ref[part].astype(F32)
        total = total + jnp.sum(block * block, keepdims=True)
        units = lax.broadcasted_iota(jnp.int32, (own, count), 0) + part * own
        picks = (units == chosen).astype(F32).astype(BF16)
        removed = removed + dot(every_ref[part], picks)
        gone = dot(jnp.ones((8, count), BF16), picks, 1, 1)[:1]
        kept = (block * (1.0 - gone)).astype(BF16)
        gram = gram + dot(kept, kept, 1, 1)
    shift = total * (DAMPING / order) + 1e-6
    bound = total + shift
    inverse_bound = 1.0 / bound
    eye = (
        lax.broadcasted_iota(jnp.int32, (rows, rows), 0)
        == lax.broadcasted_iota(jnp.int32, (rows, rows), 1)
    ).astype(F32)
    gram = (gram + shift * eye) * inverse_bound
    lowest = 0.99 * (DAMPING / order) / (1.0 + DAMPING / order)
    steps = scales(lowest, ROUNDS)
    gh, gl = split(gram)
    x = 2.0 * steps[0] * eye - steps[0] ** 2 * gram
    for k in range(1, ROUNDS):
        scale = steps[k]
        if k <= SINGLE:
            xh = x.astype(BF16)
            z = dot(xh, dot(gh, xh).astype(BF16))
        else:
            xh, xl = split(x)
            yh, yl = split(three(gh, gl, xh, xl))
            z = three(xh, xl, yh, yl)
        x = 2.0 * scale * x - scale ** 2 * z
    xh, xl = split(x)
    rh = removed.astype(BF16)
    w = dot(xh, rh) + dot(xl, rh)
    wh, wl = split(w)
    rest = (removed - three(gh, gl, wh, wl)).astype(BF16)
    w = (w + dot(xh, rest)) * inverse_bound
    wh, wl = split(w)
    me = lax.axis_index("tensor")
    mine = every_ref[me]
    units = lax.broadcasted_iota(jnp.int32, (own, count), 0) + me * own
    keep = 1.0 - jnp.sum((units == chosen).astype(F32), axis=1, keepdims=True)
    mixing = (dot(mine, wh, 0, 0) + dot(mine, wl, 0, 0)) * keep
    high, low = split(mixing)
    mix_ref[0] = high
    mix_ref[1] = low


def solve(every, chosen):
    own = every.shape[2]
    whole = pl.BlockSpec(memory_space=pltpu.VMEM)
    return pl.pallas_call(
        solve_kernel,
        out_shape=jax.ShapeDtypeStruct((2, own, chosen.shape[1]), BF16),
        in_specs=[whole, whole],
        out_specs=whole,
        compiler_params=pltpu.CompilerParams(vmem_limit_bytes=48 * 2**20),
    )(every, chosen)


def final_kernel(mix_ref, chosen_ref, down_ref, dropped_ref, out_ref):
    own, count = mix_ref.shape[1:]
    units = lax.broadcasted_iota(jnp.int32, (own, count), 0) + lax.axis_index("tensor") * own
    keep = 1.0 - jnp.sum((units == chosen_ref[...]).astype(F32), axis=1, keepdims=True)
    dropped = dropped_ref[...]
    change = dot(mix_ref[0], dropped) + dot(mix_ref[1], dropped)
    out_ref[...] = ((down_ref[...].astype(F32) + change) * keep).astype(BF16)


def finish(mix, chosen, down, dropped):
    own, width = down.shape
    count = dropped.shape[0]
    tile = 512 if width % 512 == 0 else width
    return pl.pallas_call(
        final_kernel,
        grid=(width // tile,),
        out_shape=jax.ShapeDtypeStruct((own, width), BF16),
        in_specs=[
            pl.BlockSpec(mix.shape, lambda i: (0, 0, 0)),
            pl.BlockSpec(chosen.shape, lambda i: (0, 0)),
            pl.BlockSpec((own, tile), lambda i: (0, i)),
            pl.BlockSpec((count, tile), lambda i: (0, i)),
        ],
        out_specs=pl.BlockSpec((own, tile), lambda i: (0, i)),
    )(mix, chosen, down, dropped)


def local(tokens, routes, gate_weight, up_weight, down_weight, removed):
    groups = lax.axis_size("expert")
    parts = lax.axis_size("tensor")
    me = lax.axis_index("tensor")
    experts = groups * gate_weight.shape[0]
    tok_rows, width = tokens.shape
    top = routes.shape[1]
    capacity = min(tok_rows, max(2, 2 * tok_rows * top // experts))
    down = down_weight[0]
    own_rows = down.shape[0]
    chosen = removed
    units = jnp.arange(own_rows, dtype=jnp.int32)[:, None] + me * own_rows
    own_picks = (units == chosen).astype(BF16)
    term = jnp.dot(own_picks.T, down, preferred_element_type=F32)
    dropped = lax.psum(term.astype(BF16), "tensor")

    placing = placing_matrix(routes, experts, capacity)
    share = width // parts
    mine = lax.dynamic_slice_in_dim(tokens, me * share, share, 1)
    outgoing = jnp.dot(placing, mine, preferred_element_type=F32).astype(BF16)
    outgoing = outgoing.reshape(experts, capacity, share)
    arrived = lax.all_to_all(outgoing, "expert", split_axis=0, concat_axis=0, tiled=True)
    pieces = lax.all_gather(arrived.reshape(experts * capacity, share), "tensor", axis=0)
    gate = jnp.zeros((experts * capacity, own_rows), F32)
    up = gate
    for part in range(parts):
        at = slice(part * share, (part + 1) * share)
        gate = gate + jnp.dot(pieces[part], gate_weight[0, at], preferred_element_type=F32)
        up = up + jnp.dot(pieces[part], up_weight[0, at], preferred_element_type=F32)
    hidden = (jax.nn.silu(gate) * up).astype(BF16)
    every = lax.all_gather(hidden, "tensor", axis=0)
    mix = solve(every, chosen)
    return finish(mix, chosen, down, dropped)[None]


def solution(mesh):
    in_specs = (
        P("expert", None),
        P("expert", None),
        P("expert", None, "tensor"),
        P("expert", None, "tensor"),
        P("expert", "tensor", None),
        P("expert", None),
    )
    out_specs = P("expert", "tensor", None)
    return jax.shard_map(local, mesh=mesh, in_specs=in_specs, out_specs=out_specs, check_vma=False)
```

time: 691 us -> 257 us (0.37); the launches traced: 682 us -> 257 us
  other arithmetic: 323 us -> 1.01 us
  waiting for transfers between devices: 22 us -> 144 us
  blocking collectives: 176 us -> 57.2 us
  local copies, waits for them, and re-layouts: 70.6 us -> 3.22 us
  matrix products: 68.5 us -> 15 us
  Pallas kernels: 0 us -> 22.7 us
  between operations: 21.7 us -> 13.3 us
    another operation x45 -> x2, other arithmetic: 315 us -> 0.65 us  [the longest x30 173 us: local(): lower = jnp.linalg.cholesky(damped)]
    all_to_all x1, blocking collectives: 176 us -> 57.2 us  [local(): lax.all_to_all(outgoing, 'expert', split_axis=0, concat_axis=0, tiled=True)]
    all_gather x1 -> x2, waiting for transfers between devices: 22 us -> 99 us  [the longest x1 74.7 us: local(): lax.all_gather(arrived.reshape(experts * capacity, share), 'tensor', axis=0)]
    another operation x52 -> x0, matrix products: 50.2 us -> none  [the longest x14 24.1 us: local(): lower = jnp.linalg.cholesky(damped)]
    psum x1, waiting for transfers between devices: 0.02 us -> 45.1 us  [local(): dropped = lax.psum(term.astype(BF16), 'tensor')]
    another operation x55 -> x1, local copies, waits for them, and re-layouts: 38.5 us -> 0.01 us
    pallas_call x0 -> x2, Pallas kernels: none -> 22.7 us  [the longest x1 16.2 us: solve(): pl.pallas_call(solve_kernel, out_shape=jax.ShapeDtypeStruct((2, own, chos...]
    gather x3 -> x0, local copies, waits for them, and re-layouts: 20.2 us -> none  [the longest x1 17.5 us: local(): shift = DAMPING * jnp.mean(jnp.diagonal(gram)) + 1e-06]
  transfers between devices with their start and end apart: 2 -> 3, of which waited for: 1 -> 3; matrix products, arithmetic and copies ran while one was open for 65% -> 1% of each run, Pallas kernels for 0% -> 6%
where the time goes in v1:
time: 257 us
  waiting for transfers between devices  144 us (56%)
  blocking collectives  57.2 us (22%)
  Pallas kernels  22.7 us (9%)
  matrix products  15 us (6%)
  between operations  13.3 us (5%)
  local copies, waits for them, and re-layouts  3.22 us (1%)
    all_gather x1, waiting for transfers between devices, local(): lax.all_gather(arrived.reshape(experts * capacity, share), 'tensor', axis=0)  74.7 us
    all_to_all x1, blocking collectives, local(): lax.all_to_all(outgoing, 'expert', split_axis=0, concat_axis=0, tiled=True)  57.2 us
    psum x1, waiting for transfers between devices, local(): dropped = lax.psum(term.astype(BF16), 'tensor')  45.1 us
    all_gather x1, waiting for transfers between devices, local(): every = lax.all_gather(hidden, 'tensor', axis=0)  24.4 us
    pallas_call x1, Pallas kernels, solve(): pl.pallas_call(solve_kernel, out_shape=jax.ShapeDtypeStruct((2, own, chos...  16.2 us
    dot_general x4, matrix products, local(): jnp.dot(pieces[part], gate_weight[0, at], preferred_element_type=F32)  9.08 us
    pallas_call x1, Pallas kernels, finish(): pl.pallas_call(final_kernel, grid=(width // tile,), out_shape=jax.ShapeDt...  6.58 us
  transfers between devices with their start and end apart: 3, of which 3 were waited for; matrix products, arithmetic and copies ran while one was open for 1% of the time, Pallas kernels for 6%

profile of v1, /device:TPU:1, one launch (start us, length us, event | category | flops | bytes accessed | tf_op | source)
XLA Modules:
  0.0 256.9 jit_solution(1749830012926204368)
XLA Ops:
  6.5 0.8 copy.16
  7.6 0.6 reduce-window.6
  8.2 0.2 slice_reduce_fusion
  8.4 0.1 fusion.39
  8.6 0.2 convert_reduce_fusion
  8.9 0.7 fusion
  9.5 57.2 %all_to_all.5 = bf16[64,8,1792]{2,1,0:T(8,128)(2,1)} all-to-all(bf16[64,8,1792]{2,1,0:T(8,128)(2,1)S(1)} %fusion), channel_id=1, replica_groups=mesh['expert'=64,'tensor'=4] {'expert'}, dimensions={0} | all-to-all | bytes 3670016 | tf_op jit(solution)/shard_map/all_to_all | solution.py:168
  66.8 74.7 %all-gather.4.cloned.1.call-done = bf16[4,512,1792]{2,1,0:T(8,128)(2,1)} async-done(((bf16[1,512,1792]{2,1,0:T(8,128)(2,1)}), bf16[4,512,1792]{2,1,0:T(8,128)(2,1)}) %all-gather.4.cloned.1.call-update) | async-done | bytes 7340048 | tf_op jit(solution)/shard_map/all_gather | solution.py:169
  141.4 2.5 fusion.2
  144.0 2.8 %fusion.14 = f32[512,256]{1,0:T(8,128)S(1)} fusion(f32[512,256]{1,0:T(8,128)S(1)} %fusion.2, bf16[4,512,1792]{2,1,0:T(8,128)(2,1)} %all-gather.4.cloned.1.call-done, bf16[1,7168,256]{2,1,0:T(8,128)(2,1)} %param.8), kind=kOutput, calls=%fused_computation.20 | convolution fusion | flops 469893120 | bytes 3801088 | tf_op jit(solution)/shard_map/dot_general | solution.py:174
  146.8 2.0 fusion.12
  148.7 1.8 fusion.9
  150.6 0.6 fusion.1
  151.2 0.6 fusion.15
  151.9 0.6 fusion.13
  152.6 1.4 fusion.16
  153.9 0.2 all-reduce.2.cloned.1.call-start
  154.2 2.0 convolution_convert_fusion
  156.2 24.4 %all-gather.6.cloned.1.call-done = bf16[2048,256]{1,0:T(8,128)(2,1)} async-done(((bf16[512,256]{1,0:T(8,128)(2,1)}), bf16[2048,256]{1,0:T(8,128)(2,1)}) %all-gather.6.cloned.1.call-update) | async-done | bytes 1048592 | tf_op jit(solution)/shard_map/all_gather | solution.py:177
  180.6 1.2 copy-done.1
  181.8 16.2 %shard_map.64.mix_ref = bf16[2,256,256]{2,1,0:T(8,128)(2,1)S(1)} custom-call(bf16[4,512,256]{2,1,0:T(8,128)(2,1)S(1)} %bitcast.85, s32[1,256]{1,0:T(1,128)S(1)} %copy-done.3), custom_call_target="tpu_custom_call" | custom-call | tf_op jit(solution)/shard_map/pallas_call | solution.py:111
  198.0 0.7 copy-done.2
  198.7 45.1 %all-reduce.2.cloned.1.call-done.dropped_ref = bf16[256,3584]{1,0:T(8,128)(2,1)} async-done(((bf16[256,3584]{1,0:T(8,128)(2,1)}), bf16[256,3584]{1,0:T(8,128)(2,1)}) %all-reduce.2.cloned.1.call-update) | async-done | bytes 1835024 | tf_op jit(solution)/shard_map/psum | solution.py:161
  243.8 6.6 %shard_map.65 = bf16[256,3584]{1,0:T(8,128)(2,1)} custom-call(bf16[2,256,256]{2,1,0:T(8,128)(2,1)} %copy-done.2, s32[1,256]{1,0:T(1,128)} %chosen_ref.3, bf16[256,3584]{1,0:T(8,128)(2,1)} %bitcast.88, bf16[256,3584]{1,0:T(8,128)(2,1)} %all-reduce.2.cloned.1.call-done.dropped_ref), custom_call_target="tpu_custom_call" | custom-call | tf_op jit(solution)/shard_map/pallas_call | solution.py:133
  (25 shorter events, 0.4 us)
Async XLA Ops:
  6.5 2.3 copy-start
  6.5 134.9 %all-gather.4.cloned.1.call-start = ((), (), s32[]{:S(2)}) async-start(), calls=%async_computation.1 | async-start | bytes 9175040 | tf_op jit(solution)/shard_map/all_gather | solution.py:169
  66.7 113.9 %all-gather.6.cloned.1.call-start = ((), (), s32[]{:S(2)}) async-start(), calls=%async_computation.3 | async-start | bytes 1310720 | tf_op jit(solution)/shard_map/all_gather | solution.py:177
  141.4 5.3 %copy-start.5 = (bf16[4,512,1792]{2,1,0:T(8,128)(2,1)S(1)}, bf16[4,512,1792]{2,1,0:T(8,128)(2,1)}, u32[]{:S(2)}) copy-start(bf16[4,512,1792]{2,1,0:T(8,128)(2,1)} %all-gather.4.cloned.1.call-done) | copy-start | bytes 22020100
  146.7 3.8 %copy-start.6 = (bf16[1,7168,256]{2,1,0:T(8,128)(2,1)S(1)}, bf16[1,7168,256]{2,1,0:T(8,128)(2,1)}, u32[]{:S(2)}) copy-start(bf16[1,7168,256]{2,1,0:T(8,128)(2,1)} %param.9) | copy-start | bytes 11010052
  152.5 1.7 copy-start.3
  152.5 1.7 copy-start.4
  153.9 89.9 %all-reduce.2.cloned.1.call-start = ((), (), s32[]{:S(2)}) async-start(), calls=%async_computation.2 | async-start | bytes 3670016 | tf_op jit(solution)/shard_map/psum | solution.py:161
  180.6 1.2 copy-start.1
  198.0 0.7 copy-start.2
Sparse Core Ops, SparseCore 0:
  66.8 74.5 all-gather.3
  154.1 26.4 all-gather.5
  183.0 60.8 all-reduce.1

commit v2 on v1

--- a/solution.py
+++ b/solution.py
@@ -1,5 +1,3 @@
-import functools
-
 import jax
 import jax.numpy as jnp
 from jax import lax
@@ -13,18 +11,6 @@
 SINGLE = 2
 ROUNDS = 9
 CAP = 1.85
-
-
-def placing_matrix(routes, experts, capacity):
-    tok_rows, top = routes.shape
-    flat = routes.reshape(-1)
-    onehot = (flat[:, None] == jnp.arange(experts, dtype=jnp.int32)[None, :]).astype(jnp.int32)
-    before = jnp.cumsum(onehot, axis=0) - onehot
-    slot_in = jnp.sum(before * onehot, axis=1)
-    target = (flat * capacity + slot_in).reshape(tok_rows, top)
-    slots = jnp.arange(experts * capacity, dtype=jnp.int32)
-    hits = target[None, :, :] == slots[:, None, None]
-    return jnp.sum(hits.astype(F32), axis=2).astype(BF16)
 
 
 def dot(a, b, left=1, right=0):
@@ -144,14 +130,276 @@
     )(mix, chosen, down, dropped)
 
 
+ZS, XS = 8, 4
+CHIPS = ZS * XS
+CORES = 2
+MOST = 8
+MESH = pl.DeviceIdType.MESH
+
+
+def ring_place(cycle, z, x):
+    if cycle == 0:
+        return 4 * z + lax.rem(x + z, 4)
+    t = lax.rem(z + 5 * x, 8)
+    return 4 * (x + 4 * (t // 4)) + lax.rem(t, 4)
+
+
+def ring_chip(cycle, place):
+    if cycle == 0:
+        z = place // 4
+        x = lax.rem(lax.rem(place, 4) + 3 * z, 4)
+    else:
+        r = place // 4
+        x = lax.rem(r, 4)
+        z = lax.rem(3 * r + lax.rem(place, 4), 8)
+    return z * XS + x
+
+
+def dispatch_kernel(
+    tok_ref, route_ref, gate_ref, up_ref, every_ref,
+    held, told, rows, other, gate_w, up_w, gate_sum, up_sum, hidden,
+    ring_send, ring_recv, told_send, told_recv, rows_recv, sib_send, y_send, y_sib_send,
+    pre_send, pre_recv, local_sem, weight_sem, hid_send, hid_recv,
+):
+    index = lax.axis_index("expert")
+    t = lax.axis_index("tensor")
+    core = lax.rem(index, 2)
+    chip = index // 2
+    z, x = chip // XS, lax.rem(chip, XS)
+    half = lax.rem(t, 2)
+    mate = chip * 2 + 1 - core
+    above, below, across = lax.rem(t + 1, 4), lax.rem(t + 3, 4), lax.rem(t + 2, 4)
+    places = [ring_place(c, z, x) for c in range(2)]
+    nexts = [ring_chip(c, lax.rem(places[c] + 1, CHIPS)) * 2 + core for c in range(2)]
+    prevs = [ring_chip(c, lax.rem(places[c] + CHIPS - 1, CHIPS)) * 2 + core for c in range(2)]
+    tok_rows = tok_ref.shape[0]
+    wide = held.shape[-1]
+
+    loads = [
+        pltpu.make_async_copy(gate_ref.at[0], gate_w, weight_sem.at[0]),
+        pltpu.make_async_copy(up_ref.at[0], up_w, weight_sem.at[1]),
+    ]
+    for load in loads:
+        load.start()
+
+    barrier = pltpu.get_barrier_semaphore()
+    partners = [(n, t) for n in nexts + prevs] + [(mate, t)]
+    partners += [(e, y) for e in (index, mate) for y in (above, below)] + [(index, across)]
+    for partner in partners:
+        pl.semaphore_signal(barrier, inc=1, device_id=partner, device_id_type=MESH)
+    pl.semaphore_wait(barrier, len(partners))
+
+    def remote(src, dst, send, recv, to):
+        return pltpu.make_async_remote_copy(
+            src_ref=src, dst_ref=dst, send_sem=send, recv_sem=recv, device_id=to, device_id_type=MESH
+        )
+
+    def columns(of_core, cycle):
+        first = half * (4 * wide) + of_core * (2 * wide) + cycle * wide
+        return pl.ds(pl.multiple_of(first, 128), wide)
+
+    band = pl.ds(pl.multiple_of(core * tok_rows, 32), tok_rows)
+    first = []
+    for c in range(2):
+        first.append(
+            remote(
+                tok_ref.at[:, columns(1 - core, c)], held.at[c, places[c], band],
+                pre_send.at[c], pre_recv.at[c], (mate, t),
+            )
+        )
+        first.append(
+            remote(
+                route_ref, told.at[c, places[c], core],
+                pre_send.at[2 + c], pre_recv.at[2 + c], (mate, t),
+            )
+        )
+    for copy in first:
+        copy.start()
+    own = []
+    for c in range(2):
+        own.append(
+            pltpu.make_async_copy(
+                tok_ref.at[:, columns(core, c)], held.at[c, places[c], band], local_sem.at[c]
+            )
+        )
+        own.append(
+            pltpu.make_async_copy(route_ref, told.at[c, places[c], core], local_sem.at[2 + c])
+        )
+    for copy in own:
+        copy.start()
+    for copy in own:
+        copy.wait()
+    for copy in first:
+        copy.wait()
+
+    def place_at(c, way, step):
+        if way == 0:
+            return lax.rem(places[c] + CHIPS - step, CHIPS)
+        return lax.rem(places[c] + step, CHIPS)
+
+    def send(c, way, step):
+        at = place_at(c, way, step)
+        to = ((nexts if way == 0 else prevs)[c], t)
+        remote(
+            held.at[c, at], held.at[c, at], ring_send.at[c, way], ring_recv.at[c, way, step + 1], to
+        ).start()
+        remote(
+            told.at[c, at], told.at[c, at], told_send.at[c, way], told_recv.at[c, way, step + 1], to
+        ).start()
+
+    def take(c, way, step):
+        at = place_at(c, way, step)
+        to = ((nexts if way == 0 else prevs)[c], t)
+        remote(
+            held.at[c, at], held.at[c, at], ring_send.at[c, way], ring_recv.at[c, way, step], to
+        ).wait_recv()
+        remote(
+            told.at[c, at], told.at[c, at], told_send.at[c, way], told_recv.at[c, way, step], to
+        ).wait_recv()
+
+    lane = lax.broadcasted_iota(jnp.int32, (128, 128), 1)
+    earlier = (lax.broadcasted_iota(jnp.int32, (128, 128), 0) < lane).astype(F32).astype(BF16)
+    slot = lax.rem(lax.broadcasted_iota(jnp.int32, (4 * MOST, 128), 0), MOST).astype(F32)
+
+    def pick(events):
+        marks = []
+        for c, at in events:
+            for expert in (index, mate):
+                for h in range(CORES):
+                    named = (told[c, at, h] == expert).astype(F32)
+                    marks.append(jnp.broadcast_to(jnp.sum(named, axis=0, keepdims=True), (MOST, 128)))
+        marks = jnp.concatenate(marks, axis=0)
+        ranks = dot(marks.astype(BF16), earlier)
+        out = []
+        for n, (c, at) in enumerate(events):
+            part = slice(n * 4 * MOST, (n + 1) * 4 * MOST)
+            hits = jnp.where(ranks[part] == slot, marks[part], 0.0)[:, : CORES * tok_rows]
+            out.append(dot(hits.astype(BF16), held[c, at]).astype(BF16))
+        for (c, at), block in zip(events, out):
+            source = ring_chip(c, at)
+            rows[half * 4 + core * 2 + c, source] = block[: 2 * MOST]
+            other[c, source] = block[2 * MOST :]
+        for c, at in events:
+            source = ring_chip(c, at)
+            piece = half * 4 + core * 2 + c
+            y = above if c == 0 else below
+            target = rows.at[piece, source]
+            got = rows_recv.at[piece]
+            remote(other.at[c, source], target, y_sib_send.at[c], got, (mate, y)).start()
+            remote(rows.at[piece, source], target, y_send.at[c], got, (index, y)).start()
+            remote(other.at[c, source], target, sib_send.at[c], got, (mate, t)).start()
+
+    for c in range(2):
+        for way in range(2):
+            send(c, way, 0)
+    pick([(c, places[c]) for c in range(2)])
+
+    def turn(step, carry):
+        for c in range(2):
+            for way in range(2):
+                take(c, way, step)
+                if way == 0:
+                    send(c, way, step)
+                else:
+                    @pl.when(step < CHIPS // 2 - 1)
+                    def _():
+                        send(c, way, step)
+        pick([(c, place_at(c, way, step)) for c in range(2) for way in range(2)])
+        return carry
+
+    lax.fori_loop(1, CHIPS // 2, turn, 0)
+    for c in range(2):
+        take(c, 0, CHIPS // 2)
+    pick([(c, place_at(c, 0, CHIPS // 2)) for c in range(2)])
+
+    for load in loads:
+        load.wait()
+    gate_sum[...] = jnp.zeros_like(gate_sum)
+    up_sum[...] = jnp.zeros_like(up_sum)
+
+    def multiply(piece):
+        at = pl.ds(pl.multiple_of(piece * wide, 128), wide)
+        block = rows[piece].reshape(CHIPS * 2 * MOST, wide)
+        gate_sum[...] += dot(block, gate_w[at, :])
+        up_sum[...] += dot(block, up_w[at, :])
+
+    def piece_step(n, carry):
+        kind, c = n // 2, lax.rem(n, 2)
+        near = n < 4
+        whose = jnp.where(near, jnp.where(n < 2, core, 1 - core), kind - 2)
+        piece = jnp.where(near, half, 1 - half) * 4 + whose * 2 + c
+
+        @pl.when(n >= 2)
+        def _():
+            remote(
+                rows.at[piece], rows.at[piece], sib_send.at[0], rows_recv.at[piece], (mate, t)
+            ).wait_recv()
+
+        multiply(piece)
+        return carry
+
+    lax.fori_loop(0, 8, piece_step, 0)
+    gate = gate_sum[...]
+    hidden[t] = (gate / (1.0 + jnp.exp(-gate)) * up_sum[...]).astype(BF16)
+    copies = [
+        remote(hidden.at[t], hidden.at[t], hid_send.at[n], hid_recv.at[n], (index, y))
+        for n, y in enumerate((across, above, below))
+    ]
+    for copy in copies:
+        copy.start()
+    for c in range(2):
+        for way in range(2):
+            count = CHIPS // 2 - way
+            gone = held.at[c, pl.ds(0, count)]
+            remote(gone, gone, ring_send.at[c, way], ring_recv.at[c, way, 0], (mate, t)).wait_send()
+            gone = told.at[c, pl.ds(0, count)]
+            remote(gone, gone, told_send.at[c, way], told_recv.at[c, way, 0], (mate, t)).wait_send()
+        whole = other.at[c]
+        for sem in (sib_send, y_send, y_sib_send):
+            remote(whole, whole, sem.at[c], rows_recv.at[0], (mate, t)).wait_send()
+    for copy in copies:
+        copy.wait()
+    every_ref[...] = hidden[...]
+
+
+def dispatch(tokens, told, gate_weight, up_weight):
+    tok_rows, width = tokens.shape
+    own = gate_weight.shape[2]
+    wide = width // 8
+    slots = CHIPS * 2 * MOST
+    whole = pl.BlockSpec(memory_space=pltpu.VMEM)
+    left = pl.BlockSpec(memory_space=pl.ANY)
+    dma = pltpu.SemaphoreType.DMA
+    return pl.pallas_call(
+        dispatch_kernel,
+        out_shape=jax.ShapeDtypeStruct((4, slots, own), BF16),
+        in_specs=[whole, whole, left, left],
+        out_specs=whole,
+        scratch_shapes=[
+            pltpu.VMEM((2, CHIPS, CORES * tok_rows, wide), BF16),
+            pltpu.VMEM((2, CHIPS, CORES, 8, 128), jnp.int32),
+            pltpu.VMEM((8, CHIPS, 2 * MOST, wide), BF16),
+            pltpu.VMEM((2, CHIPS, 2 * MOST, wide), BF16),
+            pltpu.VMEM((width, own), BF16),
+            pltpu.VMEM((width, own), BF16),
+            pltpu.VMEM((slots, own), F32),
+            pltpu.VMEM((slots, own), F32),
+            pltpu.VMEM((4, slots, own), BF16),
+            dma((2, 2)), dma((2, 2, 17)), dma((2, 2)), dma((2, 2, 17)), dma((8,)), dma((2,)), dma((2,)),
+            dma((2,)), dma((4,)), dma((4,)), dma((4,)), dma((2,)), dma((3,)), dma((3,)),
+        ],
+        compiler_params=pltpu.CompilerParams(
+            collective_id=0, has_side_effects=True, vmem_limit_bytes=48 * 2**20
+        ),
+        cost_estimate=pl.CostEstimate(
+            flops=4 * slots * width * own, bytes_accessed=4 * width * own, transcendentals=slots * own
+        ),
+    )(tokens, told, gate_weight, up_weight)
+
+
 def local(tokens, routes, gate_weight, up_weight, down_weight, removed):
-    groups = lax.axis_size("expert")
-    parts = lax.axis_size("tensor")
     me = lax.axis_index("tensor")
-    experts = groups * gate_weight.shape[0]
-    tok_rows, width = tokens.shape
-    top = routes.shape[1]
-    capacity = min(tok_rows, max(2, 2 * tok_rows * top // experts))
+    tok_rows, top = routes.shape
     down = down_weight[0]
     own_rows = down.shape[0]
     chosen = removed
@@ -159,22 +407,11 @@
     own_picks = (units == chosen).astype(BF16)
     term = jnp.dot(own_picks.T, down, preferred_element_type=F32)
     dropped = lax.psum(term.astype(BF16), "tensor")
-
-    placing = placing_matrix(routes, experts, capacity)
-    share = width // parts
-    mine = lax.dynamic_slice_in_dim(tokens, me * share, share, 1)
-    outgoing = jnp.dot(placing, mine, preferred_element_type=F32).astype(BF16)
-    outgoing = outgoing.reshape(experts, capacity, share)
-    arrived = lax.all_to_all(outgoing, "expert", split_axis=0, concat_axis=0, tiled=True)
-    pieces = lax.all_gather(arrived.reshape(experts * capacity, share), "tensor", axis=0)
-    gate = jnp.zeros((experts * capacity, own_rows), F32)
-    up = gate
-    for part in range(parts):
-        at = slice(part * share, (part + 1) * share)
-        gate = gate + jnp.dot(pieces[part], gate_weight[0, at], preferred_element_type=F32)
-        up = up + jnp.dot(pieces[part], up_weight[0, at], preferred_element_type=F32)
-    hidden = (jax.nn.silu(gate) * up).astype(BF16)
-    every = lax.all_gather(hidden, "tensor", axis=0)
+    core = lax.rem(lax.axis_index("expert"), CORES)
+    told = lax.dynamic_update_slice(
+        jnp.full((top, 128), -1, jnp.int32), routes.T, (0, core * tok_rows)
+    )
+    every = dispatch(tokens, told, gate_weight, up_weight)
     mix = solve(every, chosen)
     return finish(mix, chosen, down, dropped)[None]
 

time: 257 us -> 151 us (0.59)
  waiting for transfers between devices: 144 us -> 0.02 us
  Pallas kernels: 22.7 us -> 130 us
  blocking collectives: 57.2 us -> 0 us
  matrix products: 15 us -> 3.5 us
    pallas_call x0 -> x1, Pallas kernels: none -> 108 us  [dispatch(): pl.pallas_call(dispatch_kernel, out_shape=jax.ShapeDtypeStruct((4, slots,...]
    all_gather x2 -> x0, waiting for transfers between devices: 99 us -> none  [the longest x1 74.7 us: local(): lax.all_gather(arrived.reshape(experts * capacity, share), 'tensor', axis=0)]
    all_to_all x1 -> x0, blocking collectives: 57.2 us -> none  [local(): lax.all_to_all(outgoing, 'expert', split_axis=0, concat_axis=0, tiled=True)]
    psum x1, waiting for transfers between devices: 45.1 us -> 0.01 us  [local(): dropped = lax.psum(term.astype(BF16), 'tensor')]
    dot_general x9 -> x0, matrix products: 13 us -> none  [the longest x4 9.08 us: local(): jnp.dot(pieces[part], gate_weight[0, at], preferred_element_type=F32)]
  transfers between devices with their start and end apart: 3 -> 1, of which waited for: 3 -> 0; matrix products, arithmetic and copies ran while one was open for 1% -> 0% of each run, Pallas kernels for 6% -> 82%
where the time goes in v2:
time: 151 us
  Pallas kernels  130 us (86%)
  between operations  13.4 us (9%)
  local copies, waits for them, and re-layouts  3.72 us (2%)
  matrix products  3.5 us (2%)
    pallas_call x1, Pallas kernels, dispatch(): pl.pallas_call(dispatch_kernel, out_shape=jax.ShapeDtypeStruct((4, slots,...  108 us
    pallas_call x1, Pallas kernels, solve(): pl.pallas_call(solve_kernel, out_shape=jax.ShapeDtypeStruct((2, own, chos...  16.1 us
    pallas_call x1, Pallas kernels, finish(): pl.pallas_call(final_kernel, grid=(width // tile,), out_shape=jax.ShapeDt...  6.58 us
    unnamed x10, local copies, waits for them, and re-layouts  3.55 us
    dot_general x1, matrix products, local(): term = jnp.dot(own_picks.T, down, preferred_element_type=F32)  3.5 us
  transfers between devices with their start and end apart: 1, of which 0 were waited for; matrix products, arithmetic and copies ran while one was open for 0% of the time, Pallas kernels for 82%

profile of v2, /device:TPU:1, one launch (start us, length us, event | category | flops | bytes accessed | tf_op | source)
XLA Modules:
  0.0 151.0 jit_solution(14562109343026545777)
XLA Ops:
  6.5 0.0 all-reduce.2.cloned.1.call-start
  6.5 3.5 %convolution_convert_fusion = bf16[256,3584]{1,0:T(8,128)(2,1)} fusion(s32[256]{0:T(256)} %bitcast.6, s32[256]{0:T(256)S(1)} %iota_add_fusion, bf16[1,256,3584]{2,1,0:T(8,128)(2,1)} %param.10), kind=kOutput, calls=%fused_computation | convolution fusion | flops 470745088 | bytes 3672064 | tf_op jit(solution)/shard_map/dot_general | solution.py:408
  10.0 0.0 copy-start.4
  10.0 0.0 copy-start.3
  10.1 0.0 all-reduce.2.cloned.1.call-update
  10.1 0.6 copy-done.4
  10.7 0.2 dynamic_update_slice.3.route_ref
  10.9 0.2 copy-done.3
  11.1 0.0 copy-start.2
  11.1 2.0 %copy-done.2 = bf16[1,7168,256]{2,1,0:T(8,128)(2,1)S(1)} copy-done((bf16[1,7168,256]{2,1,0:T(8,128)(2,1)S(1)}, bf16[1,7168,256]{2,1,0:T(8,128)(2,1)}, u32[]{:S(2)}) %copy-start.2) | copy-done | bytes 3670040
  13.1 0.0 copy-start.1
  13.1 107.6 %shard_map.64.every_ref = bf16[4,512,256]{2,1,0:T(8,128)(2,1)S(1)} custom-call(bf16[32,7168]{1,0:T(8,128)(2,1)S(1)} %copy-done.3, s32[8,128]{1,0:T(8,128)S(1)} %dynamic_update_slice.3.route_ref, bf16[1,7168,256]{2,1,0:T(8,128)(2,1)S(1)} %copy-done.2, bf16[1,7168,256]{2,1,0:T(8,128)(2,1)} %up_ref.1), custom_call_target="tpu_custom_call" | custom-call | flops 3758096384 | bytes 7340032 | tf_op jit(solution)/shard_map/pallas_call | solution.py:373
  120.7 0.0 copy-done.1
  120.7 16.1 %shard_map.65.mix_ref = bf16[2,256,256]{2,1,0:T(8,128)(2,1)S(1)} custom-call(bf16[4,512,256]{2,1,0:T(8,128)(2,1)S(1)} %shard_map.64.every_ref, s32[1,256]{1,0:T(1,128)S(1)} %copy-done.1), custom_call_target="tpu_custom_call" | custom-call | tf_op jit(solution)/shard_map/pallas_call | solution.py:97
  136.9 0.0 copy-start
  136.9 0.7 copy-done
  137.6 0.0 all-reduce.2.cloned.1.call-done.dropped_ref
  137.6 6.6 %shard_map.66 = bf16[256,3584]{1,0:T(8,128)(2,1)} custom-call(bf16[2,256,256]{2,1,0:T(8,128)(2,1)} %copy-done, s32[1,256]{1,0:T(1,128)} %chosen_ref.3, bf16[256,3584]{1,0:T(8,128)(2,1)} %bitcast.7, bf16[256,3584]{1,0:T(8,128)(2,1)} %all-reduce.2.cloned.1.call-done.dropped_ref), custom_call_target="tpu_custom_call" | custom-call | tf_op jit(solution)/shard_map/pallas_call | solution.py:119
  (2 shorter events, 0.0 us)
Async XLA Ops:
  6.5 131.0 %all-reduce.2.cloned.1.call-start = ((), (), s32[]{:S(2)}) async-start(), calls=%async_computation | async-start | bytes 3670016 | tf_op jit(solution)/shard_map/psum | solution.py:409
  10.0 0.7 copy-start.4
  10.0 1.0 copy-start.3
  11.1 2.0 %copy-start.2 = (bf16[1,7168,256]{2,1,0:T(8,128)(2,1)S(1)}, bf16[1,7168,256]{2,1,0:T(8,128)(2,1)}, u32[]{:S(2)}) copy-start(bf16[1,7168,256]{2,1,0:T(8,128)(2,1)} %gate_ref.1) | copy-start | bytes 11010052
  13.1 107.6 %copy-start.1 = (s32[1,256]{1,0:T(1,128)S(1)}, s32[1,256]{1,0:T(1,128)}, u32[]{:S(2)}) copy-start(s32[1,256]{1,0:T(1,128)} %chosen_ref.3) | copy-start | bytes 3076
  136.9 0.7 copy-start
Sparse Core Ops, SparseCore 0:
  10.2 90.0 all-reduce.1

commit v3 on v2

v3 whole, which is shorter than its diff:
```python
import jax
import jax.numpy as jnp
from jax import lax
from jax.experimental import pallas as pl
from jax.experimental.pallas import tpu as pltpu
from jax.sharding import PartitionSpec as P

DAMPING = 0.1
F32 = jnp.float32
BF16 = jnp.bfloat16
SINGLE = 2
ROUNDS = 9
CAP = 1.85
TILES = 7


def dot(a, b, left=1, right=0):
    return lax.dot_general(a, b, (((left,), (right,)), ((), ())), preferred_element_type=F32)


def split(x):
    high = x.astype(BF16)
    return high, (x - high.astype(F32)).astype(BF16)


def three(ah, al, bh, bl):
    return dot(ah, bh) + dot(ah, bl) + dot(al, bh)


def scales(lowest, rounds):
    out = []
    for _ in range(rounds):
        scale = min(2.0 / (1.0 + lowest), CAP)
        out.append(scale)
        lowest = 1.0 - (1.0 - scale * lowest) ** 2
    return out


def solve_kernel(
    every_ref, chosen_ref, down_ref, dropped_ref, out_ref, down, dropped, result, load_sem, store_sem
):
    loads = [
        pltpu.make_async_copy(down_ref, down, load_sem.at[0]),
        pltpu.make_async_copy(dropped_ref, dropped, load_sem.at[1]),
    ]
    for copy in loads:
        copy.start()
    parts, rows, own = every_ref.shape
    count = chosen_ref.shape[1]
    order = parts * own
    chosen = chosen_ref[...]
    total = jnp.zeros((1, 1), F32)
    removed = jnp.zeros((rows, count), F32)
    gram = jnp.zeros((rows, rows), F32)
    for part in range(parts):
        block = every_ref[part].astype(F32)
        total = total + jnp.sum(block * block, keepdims=True)
        units = lax.broadcasted_iota(jnp.int32, (own, count), 0) + part * own
        picks = (units == chosen).astype(F32).astype(BF16)
        removed = removed + dot(every_ref[part], picks)
        gone = dot(jnp.ones((8, count), BF16), picks, 1, 1)[:1]
        kept = (block * (1.0 - gone)).astype(BF16)
        gram = gram + dot(kept, kept, 1, 1)
    shift = total * (DAMPING / order) + 1e-6
    bound = total + shift
    inverse_bound = 1.0 / bound
    eye = (
        lax.broadcasted_iota(jnp.int32, (rows, rows), 0)
        == lax.broadcasted_iota(jnp.int32, (rows, rows), 1)
    ).astype(F32)
    gram = (gram + shift * eye) * inverse_bound
    lowest = 0.99 * (DAMPING / order) / (1.0 + DAMPING / order)
    steps = scales(lowest, ROUNDS)
    gh, gl = split(gram)
    x = 2.0 * steps[0] * eye - steps[0] ** 2 * gram
    for k in range(1, ROUNDS):
        scale = steps[k]
        if k <= SINGLE:
            xh = x.astype(BF16)
            z = dot(xh, dot(gh, xh).astype(BF16))
        else:
            xh, xl = split(x)
            yh, yl = split(three(gh, gl, xh, xl))
            z = three(xh, xl, yh, yl)
        x = 2.0 * scale * x - scale ** 2 * z
    xh, xl = split(x)
    rh = removed.astype(BF16)
    w = dot(xh, rh) + dot(xl, rh)
    wh, wl = split(w)
    rest = (removed - three(gh, gl, wh, wl)).astype(BF16)
    w = (w + dot(xh, rest)) * inverse_bound
    wh, wl = split(w)
    me = lax.axis_index("tensor")
    mine = every_ref[me]
    units = lax.broadcasted_iota(jnp.int32, (own, count), 0) + me * own
    keep = 1.0 - jnp.sum((units == chosen).astype(F32), axis=1, keepdims=True)
    mixing = (dot(mine, wh, 0, 0) + dot(mine, wl, 0, 0)) * keep
    high, low = split(mixing)
    for copy in loads:
        copy.wait()
    width = down_ref.shape[1]
    tile = width // TILES
    stores = []
    for n in range(TILES):
        at = slice(n * tile, (n + 1) * tile)
        part = dropped[:, at]
        change = dot(high, part) + dot(low, part)
        result[:, at] = ((down[:, at].astype(F32) + change) * keep).astype(BF16)
        stores.append(pltpu.make_async_copy(result.at[:, at], out_ref.at[:, at], store_sem.at[n]))
        stores[-1].start()
    for copy in stores:
        copy.wait()


def solve(every, chosen, down, dropped):
    own, width = down.shape
    count = chosen.shape[1]
    whole = pl.BlockSpec(memory_space=pltpu.VMEM)
    left = pl.BlockSpec(memory_space=pl.ANY)
    return pl.pallas_call(
        solve_kernel,
        out_shape=jax.ShapeDtypeStruct((own, width), BF16),
        in_specs=[whole, whole, left, left],
        out_specs=left,
        scratch_shapes=[
            pltpu.VMEM((own, width), BF16),
            pltpu.VMEM((count, width), BF16),
            pltpu.VMEM((own, width), BF16),
            pltpu.SemaphoreType.DMA((2,)),
            pltpu.SemaphoreType.DMA((TILES,)),
        ],
        compiler_params=pltpu.CompilerParams(vmem_limit_bytes=48 * 2**20),
    )(every, chosen, down, dropped)


ZS, XS = 8, 4
CHIPS = ZS * XS
CORES = 2
MOST = 8
MESH = pl.DeviceIdType.MESH


def dispatch_kernel(
    tok_ref, route_ref, gate_ref, up_ref, every_ref,
    held, told, rows, other, gate_w, up_w, gate_sum, up_sum, hidden,
    held_send, held_recv, told_send, told_recv, rows_recv, sib_send, y_send, y_sib_send,
    pre_send, pre_recv, local_sem, weight_sem, hid_send, hid_recv,
):
    index = lax.axis_index("expert")
    t = lax.axis_index("tensor")
    core = lax.rem(index, 2)
    chip = index // 2
    z, x = chip // XS, lax.rem(chip, XS)
    half = lax.rem(t, 2)
    mate = chip * 2 + 1 - core
    above, below, across = lax.rem(t + 1, 4), lax.rem(t + 3, 4), lax.rem(t + 2, 4)
    here = chip
    z_up, z_down = (lax.rem(z + 1, ZS) * XS + x) * 2 + core, (lax.rem(z + ZS - 1, ZS) * XS + x) * 2 + core
    x_up, x_down = (z * XS + lax.rem(x + 1, XS)) * 2 + core, (z * XS + lax.rem(x + XS - 1, XS)) * 2 + core
    tok_rows = tok_ref.shape[0]
    wide = held.shape[-1]

    loads = [
        pltpu.make_async_copy(gate_ref.at[0], gate_w, weight_sem.at[0]),
        pltpu.make_async_copy(up_ref.at[0], up_w, weight_sem.at[1]),
    ]
    for load in loads:
        load.start()

    barrier = pltpu.get_barrier_semaphore()
    partners = [(n, t) for n in (z_up, z_down, x_up, x_down)] + [(mate, t)]
    partners += [(e, y) for e in (index, mate) for y in (above, below)] + [(index, across)]
    for partner in partners:
        pl.semaphore_signal(barrier, inc=1, device_id=partner, device_id_type=MESH)
    pl.semaphore_wait(barrier, len(partners))

    def remote(src, dst, send, recv, to):
        return pltpu.make_async_remote_copy(
            src_ref=src, dst_ref=dst, send_sem=send, recv_sem=recv, device_id=to, device_id_type=MESH
        )

    def columns(of_core, cycle):
        first = half * (4 * wide) + of_core * (2 * wide) + cycle * wide
        return pl.ds(pl.multiple_of(first, 128), wide)

    band = pl.ds(pl.multiple_of(core * tok_rows, 32), tok_rows)
    first = []
    for c in range(2):
        first.append(
            remote(
                tok_ref.at[:, columns(1 - core, c)], held.at[c, here, band],
                pre_send.at[c], pre_recv.at[c], (mate, t),
            )
        )
    first.append(
        remote(route_ref, told.at[here, core], pre_send.at[2], pre_recv.at[2], (mate, t))
    )
    for copy in first:
        copy.start()
    own = []
    for c in range(2):
        own.append(
            pltpu.make_async_copy(
                tok_ref.at[:, columns(core, c)], held.at[c, here, band], local_sem.at[c]
            )
        )
    own.append(pltpu.make_async_copy(route_ref, told.at[here, core], local_sem.at[2]))
    for copy in own:
        copy.start()
    for copy in own:
        copy.wait()
    for copy in first:
        copy.wait()

    def at(dz, dx):
        return lax.rem(z + dz + 2 * ZS, ZS) * XS + lax.rem(x + dx + 2 * XS, XS)

    def go(c, block, to):
        remote(
            held.at[c, block], held.at[c, block], held_send.at[c], held_recv.at[c, block], (to, t)
        ).start()
        if c == 0:
            remote(
                told.at[block], told.at[block], told_send.at[0], told_recv.at[block], (to, t)
            ).start()

    def take(c, block):
        remote(
            held.at[c, block], held.at[c, block], held_send.at[c], held_recv.at[c, block], (mate, t)
        ).wait_recv()
        if c == 0:
            remote(
                told.at[block], told.at[block], told_send.at[0], told_recv.at[block], (mate, t)
            ).wait_recv()

    lane = lax.broadcasted_iota(jnp.int32, (128, 128), 1)
    earlier = (lax.broadcasted_iota(jnp.int32, (128, 128), 0) < lane).astype(F32).astype(BF16)
    slot = lax.rem(lax.broadcasted_iota(jnp.int32, (4 * MOST, 128), 0), MOST).astype(F32)

    def pick(events):
        marks = []
        for c, block in events:
            for expert in (index, mate):
                for h in range(CORES):
                    named = (told[block, h] == expert).astype(F32)
                    marks.append(jnp.broadcast_to(jnp.sum(named, axis=0, keepdims=True), (MOST, 128)))
        marks = jnp.concatenate(marks, axis=0)
        ranks = dot(marks.astype(BF16), earlier)
        out = []
        for n, (c, block) in enumerate(events):
            part = slice(n * 4 * MOST, (n + 1) * 4 * MOST)
            hits = jnp.where(ranks[part] == slot, marks[part], 0.0)[:, : CORES * tok_rows]
            out.append(dot(hits.astype(BF16), held[c, block]).astype(BF16))
        for (c, source), picked in zip(events, out):
            rows[half * 4 + core * 2 + c, source] = picked[: 2 * MOST]
            other[c, source] = picked[2 * MOST :]
        for c, source in events:
            piece = half * 4 + core * 2 + c
            y = above if c == 0 else below
            target = rows.at[piece, source]
            got = rows_recv.at[piece]
            remote(other.at[c, source], target, y_sib_send.at[c], got, (mate, y)).start()
            remote(rows.at[piece, source], target, y_send.at[c], got, (index, y)).start()
            remote(other.at[c, source], target, sib_send.at[c], got, (mate, t)).start()

    for c in range(2):
        for to in (z_up, z_down, x_up, x_down):
            go(c, here, to)
    pick([(0, here), (1, here)])

    def turn(r, carry):
        @pl.when(r <= 4)
        def _():
            block = at(-r, 0)
            take(0, block)

            @pl.when(r < 4)
            def _():
                go(0, block, z_up)

            go(0, block, x_up)
            go(0, block, x_down)

        @pl.when(r <= 3)
        def _():
            block = at(r, 0)
            take(0, block)

            @pl.when(r < 3)
            def _():
                go(0, block, z_down)

            go(0, block, x_up)
            go(0, block, x_down)

        @pl.when(r == 1)
        def _():
            block = at(0, -1)
            take(1, block)
            go(1, block, x_up)
            go(1, block, z_up)
            go(1, block, z_down)
            block = at(0, 1)
            take(1, block)
            go(1, block, z_up)
            go(1, block, z_down)

        @pl.when(r == 2)
        def _():
            block = at(0, 2)
            take(1, block)
            go(1, block, z_up)
            go(1, block, z_down)

        for dx in (0, -1, 1, 2):
            hop = r - abs(dx)
            even = lax.rem(x + dx + XS, 2) == 0
            for sign, to, most in ((-1, z_up, jnp.where(even, 4, 3)), (1, z_down, jnp.where(even, 3, 4))):
                @pl.when((hop >= 1) & (hop <= most))
                def _():
                    block = at(sign * hop, dx)
                    take(1, block)

                    @pl.when(hop < most)
                    def _():
                        go(1, block, to)

        for sign in (-1, 1):
            far = r - 1
            there = (far <= 4) if sign < 0 else (far >= 1) & (far <= 3)

            @pl.when(there)
            def _():
                even = lax.rem(z + far, 2) == 0
                block = at(sign * far, -1)
                take(0, block)

                @pl.when(even)
                def _():
                    go(0, block, x_up)

                back = at(sign * far, 1)
                take(0, back)

                @pl.when(jnp.logical_not(even))
                def _():
                    go(0, back, x_down)

        for sign in (-1, 1):
            far = r - 2
            there = (far >= 0) if sign < 0 else (far >= 1) & (far <= 3)

            @pl.when(there)
            def _():
                take(0, at(sign * far, 2))

        for dx in (0, -1, 1, 2):
            far = r - abs(dx)
            for sign in (-1, 1):
                there = (far >= 0) & (far <= 4) if sign < 0 else (far >= 1) & (far <= 3)

                @pl.when(there)
                def _():
                    block = at(sign * far, dx)
                    pick([(0, block), (1, block)])

        return carry

    lax.fori_loop(1, 7, turn, 0)

    for load in loads:
        load.wait()
    gate_sum[...] = jnp.zeros_like(gate_sum)
    up_sum[...] = jnp.zeros_like(up_sum)

    def multiply(piece, first, count):
        cut = pl.ds(pl.multiple_of(piece * wide, 128), wide)
        block = rows[piece, first : first + count].reshape(count * 2 * MOST, wide)
        span = slice(first * 2 * MOST, (first + count) * 2 * MOST)
        gate_sum[span] += dot(block, gate_w[cut, :])
        up_sum[span] += dot(block, up_w[cut, :])

    def arrived(piece):
        remote(
            rows.at[piece], rows.at[piece], sib_send.at[0], rows_recv.at[piece], (mate, t)
        ).wait_recv()

    def near(n, carry):
        piece = half * 4 + jnp.where(n < 2, core, 1 - core) * 2 + lax.rem(n, 2)

        @pl.when(n >= 2)
        def _():
            arrived(piece)

        multiply(piece, 0, CHIPS)
        return carry

    lax.fori_loop(0, 4, near, 0)
    copies = []
    middle = CHIPS // 2
    for part in range(2):
        def far(n, carry):
            piece = (1 - half) * 4 + n
            if part == 0:
                arrived(piece)
            multiply(piece, part * middle, middle)
            return carry

        lax.fori_loop(0, 4, far, 0)
        span = slice(part * middle * 2 * MOST, (part + 1) * middle * 2 * MOST)
        gate = gate_sum[span]
        hidden[t, span] = (gate / (1.0 + jnp.exp(-gate)) * up_sum[span]).astype(BF16)
        for n, y in enumerate((across, above, below)):
            mine = hidden.at[t, span]
            copies.append(
                remote(mine, mine, hid_send.at[part, n], hid_recv.at[part, n], (index, y))
            )
            copies[-1].start()
    gone = told.at[pl.ds(0, CHIPS - 1)]
    remote(gone, gone, told_send.at[0], told_recv.at[0], (mate, t)).wait_send()
    for c in range(2):
        gone = held.at[c, pl.ds(0, CHIPS - 1)]
        remote(gone, gone, held_send.at[c], held_recv.at[c, 0], (mate, t)).wait_send()
        whole = other.at[c]
        for sem in (sib_send, y_send, y_sib_send):
            remote(whole, whole, sem.at[c], rows_recv.at[0], (mate, t)).wait_send()
    for copy in copies:
        copy.wait()
    every_ref[...] = hidden[...]


def dispatch(tokens, told, gate_weight, up_weight):
    tok_rows, width = tokens.shape
    own = gate_weight.shape[2]
    wide = width // 8
    slots = CHIPS * 2 * MOST
    whole = pl.BlockSpec(memory_space=pltpu.VMEM)
    left = pl.BlockSpec(memory_space=pl.ANY)
    dma = pltpu.SemaphoreType.DMA
    return pl.pallas_call(
        dispatch_kernel,
        out_shape=jax.ShapeDtypeStruct((4, slots, own), BF16),
        in_specs=[left, whole, left, left],
        out_specs=whole,
        scratch_shapes=[
            pltpu.VMEM((2, CHIPS, CORES * tok_rows, wide), BF16),
            pltpu.VMEM((CHIPS, CORES, 8, 128), jnp.int32),
            pltpu.VMEM((8, CHIPS, 2 * MOST, wide), BF16),
            pltpu.VMEM((2, CHIPS, 2 * MOST, wide), BF16),
            pltpu.VMEM((width, own), BF16),
            pltpu.VMEM((width, own), BF16),
            pltpu.VMEM((slots, own), F32),
            pltpu.VMEM((slots, own), F32),
            pltpu.VMEM((4, slots, own), BF16),
            dma((2,)), dma((2, CHIPS)), dma((1,)), dma((CHIPS,)), dma((8,)), dma((2,)), dma((2,)),
            dma((2,)), dma((3,)), dma((3,)), dma((3,)), dma((2,)), dma((2, 3)), dma((2, 3)),
        ],
        compiler_params=pltpu.CompilerParams(
            collective_id=0, has_side_effects=True, vmem_limit_bytes=48 * 2**20
        ),
        cost_estimate=pl.CostEstimate(
            flops=4 * slots * width * own, bytes_accessed=4 * width * own, transcendentals=slots * own
        ),
    )(tokens, told, gate_weight, up_weight)


def local(tokens, routes, gate_weight, up_weight, down_weight, removed):
    me = lax.axis_index("tensor")
    tok_rows, top = routes.shape
    down = down_weight[0]
    own_rows = down.shape[0]
    chosen = removed
    units = jnp.arange(own_rows, dtype=jnp.int32)[:, None] + me * own_rows
    own_picks = (units == chosen).astype(BF16)
    term = jnp.dot(own_picks.T, down, preferred_element_type=F32)
    dropped = lax.psum(term.astype(BF16), "tensor")
    core = lax.rem(lax.axis_index("expert"), CORES)
    told = lax.dynamic_update_slice(
        jnp.full((top, 128), -1, jnp.int32), routes.T, (0, core * tok_rows)
    )
    every = dispatch(tokens, told, gate_weight, up_weight)
    return solve(every, chosen, down, dropped)[None]


def solution(mesh):
    in_specs = (
        P("expert", None),
        P("expert", None),
        P("expert", None, "tensor"),
        P("expert", None, "tensor"),
        P("expert", "tensor", None),
        P("expert", None),
    )
    out_specs = P("expert", "tensor", None)
    return jax.shard_map(local, mesh=mesh, in_specs=in_specs, out_specs=out_specs, check_vma=False)
```

time: 151 us -> 141 us (0.934)
  Pallas kernels: 130 us -> 119 us
    pallas_call x1, Pallas kernels: 108 us -> 101 us  [dispatch(): pl.pallas_call(dispatch_kernel, out_shape=jax.ShapeDtypeStruct((4, slots,...]
    pallas_call x2 -> x1, Pallas kernels: 22.7 us -> 18.5 us  [solve(): pl.pallas_call(solve_kernel, out_shape=jax.ShapeDtypeStruct((own, width),...]
    unnamed x10 -> x12, local copies, waits for them, and re-layouts: 3.55 us -> 4.36 us
  transfers between devices with their start and end apart: 1 -> 1, of which waited for: 0 -> 0; matrix products, arithmetic and copies ran while one was open for 0% -> 0% of each run, Pallas kernels for 82% -> 71%
where the time goes in v3:
time: 141 us
  Pallas kernels  119 us (84%)
  between operations  13.5 us (10%)
  local copies, waits for them, and re-layouts  4.53 us (3%)
  matrix products  3.5 us (2%)
    pallas_call x1, Pallas kernels, dispatch(): pl.pallas_call(dispatch_kernel, out_shape=jax.ShapeDtypeStruct((4, slots,...  101 us
    pallas_call x1, Pallas kernels, solve(): pl.pallas_call(solve_kernel, out_shape=jax.ShapeDtypeStruct((own, width),...  18.5 us
    unnamed x12, local copies, waits for them, and re-layouts  4.36 us
    dot_general x1, matrix products, local(): term = jnp.dot(own_picks.T, down, preferred_element_type=F32)  3.5 us
  transfers between devices with their start and end apart: 1, of which 0 were waited for; matrix products, arithmetic and copies ran while one was open for 0% of the time, Pallas kernels for 71%

profile of v3, /device:TPU:1, one launch (start us, length us, event | category | flops | bytes accessed | tf_op | source)
XLA Modules:
  0.0 140.7 jit_solution(12215496971036629658)
XLA Ops:
  6.5 0.0 all-reduce.2.cloned.1.call-start
  6.5 3.5 %convolution_convert_fusion = bf16[256,3584]{1,0:T(8,128)(2,1)} fusion(s32[256]{0:T(256)} %bitcast.7, s32[256]{0:T(256)S(1)} %iota_add_fusion, bf16[1,256,3584]{2,1,0:T(8,128)(2,1)} %param.10), kind=kOutput, calls=%fused_computation | convolution fusion | flops 470745088 | bytes 3672064 | tf_op jit(solution)/shard_map/dot_general | solution.py:475
  10.0 0.0 copy-start.5
  10.0 0.0 copy-start.4
  10.1 0.0 all-reduce.2.cloned.1.call-update
  10.1 0.6 copy-done.5
  10.7 0.2 dynamic_update_slice.3.route_ref
  10.9 0.2 copy-done.4
  11.1 0.0 copy-start.3
  11.1 2.0 %copy-done.3 = bf16[1,7168,256]{2,1,0:T(8,128)(2,1)S(1)} copy-done((bf16[1,7168,256]{2,1,0:T(8,128)(2,1)S(1)}, bf16[1,7168,256]{2,1,0:T(8,128)(2,1)}, u32[]{:S(2)}) %copy-start.3) | copy-done | bytes 3670040
  13.1 0.0 copy-start
  13.1 0.0 copy-start.2
  13.1 100.6 %shard_map.64.every_ref = bf16[4,512,256]{2,1,0:T(8,128)(2,1)S(1)} custom-call(bf16[32,7168]{1,0:T(8,128)(2,1)S(1)} %copy-done.4, s32[8,128]{1,0:T(8,128)S(1)} %dynamic_update_slice.3.route_ref, bf16[1,7168,256]{2,1,0:T(8,128)(2,1)S(1)} %copy-done.3, bf16[1,7168,256]{2,1,0:T(8,128)(2,1)} %up_ref.1), custom_call_target="tpu_custom_call" | custom-call | flops 3758096384 | bytes 7340032 | tf_op jit(solution)/shard_map/pallas_call | solution.py:440
  113.7 0.0 all-reduce.2.cloned.1.call-done.dropped_ref
  113.8 0.0 copy-done
  113.8 0.0 copy-done.2
  113.8 0.0 copy-start.1
  113.8 1.5 %copy-done.1 = bf16[256,3584]{1,0:T(8,128)(2,1)S(1)} copy-done((bf16[256,3584]{1,0:T(8,128)(2,1)S(1)}, bf16[256,3584]{1,0:T(8,128)(2,1)}, u32[]{:S(2)}) %copy-start.1) | copy-done | bytes 1835032
  115.3 18.5 %shard_map.65 = bf16[256,3584]{1,0:T(8,128)(2,1)} custom-call(bf16[4,512,256]{2,1,0:T(8,128)(2,1)S(1)} %shard_map.64.every_ref, s32[1,256]{1,0:T(1,128)S(1)} %copy-done.2, bf16[256,3584]{1,0:T(8,128)(2,1)S(1)} %bitcast.6, bf16[256,3584]{1,0:T(8,128)(2,1)S(1)} %copy-done.1), custom_call_target="tpu_custom_call" | custom-call | tf_op jit(solution)/shard_map/pallas_call | solution.py:120
  (2 shorter events, 0.0 us)
Async XLA Ops:
  6.5 107.2 %all-reduce.2.cloned.1.call-start = ((), (), s32[]{:S(2)}) async-start(), calls=%async_computation | async-start | bytes 3670016 | tf_op jit(solution)/shard_map/psum | solution.py:476
  10.0 0.7 copy-start.5
  10.0 1.0 copy-start.4
  11.1 2.0 %copy-start.3 = (bf16[1,7168,256]{2,1,0:T(8,128)(2,1)S(1)}, bf16[1,7168,256]{2,1,0:T(8,128)(2,1)}, u32[]{:S(2)}) copy-start(bf16[1,7168,256]{2,1,0:T(8,128)(2,1)} %gate_ref.1) | copy-start | bytes 11010052
  13.1 100.6 %copy-start = (bf16[1,256,3584]{2,1,0:T(8,128)(2,1)S(1)}, bf16[1,256,3584]{2,1,0:T(8,128)(2,1)}, u32[]{:S(2)}) copy-start(bf16[1,256,3584]{2,1,0:T(8,128)(2,1)} %param.10) | copy-start | bytes 5505028
  13.1 100.6 %copy-start.2 = (s32[1,256]{1,0:T(1,128)S(1)}, s32[1,256]{1,0:T(1,128)}, u32[]{:S(2)}) copy-start(s32[1,256]{1,0:T(1,128)} %chosen_ref.1) | copy-start | bytes 3076
  113.8 1.5 %copy-start.1 = (bf16[256,3584]{1,0:T(8,128)(2,1)S(1)}, bf16[256,3584]{1,0:T(8,128)(2,1)}, u32[]{:S(2)}) copy-start(bf16[256,3584]{1,0:T(8,128)(2,1)} %all-reduce.2.cloned.1.call-done.dropped_ref) | copy-start | bytes 5505028
Sparse Core Ops, SparseCore 0:
  10.2 88.5 all-reduce.1

commit v4 on v3

--- a/solution.py
+++ b/solution.py
@@ -8,10 +8,10 @@
 DAMPING = 0.1
 F32 = jnp.float32
 BF16 = jnp.bfloat16
+MESH = pl.DeviceIdType.MESH
 SINGLE = 2
 ROUNDS = 9
 CAP = 1.85
-TILES = 7
 
 
 def dot(a, b, left=1, right=0):
@@ -37,13 +37,27 @@
 
 
 def solve_kernel(
-    every_ref, chosen_ref, down_ref, dropped_ref, out_ref, down, dropped, result, load_sem, store_sem
+    every_ref, chosen_ref, down_ref, slice_ref, out_ref,
+    down, dropped, result, load_sem, store_sem, send_sem, recv_sem,
 ):
-    loads = [
-        pltpu.make_async_copy(down_ref, down, load_sem.at[0]),
-        pltpu.make_async_copy(dropped_ref, dropped, load_sem.at[1]),
+    index = lax.axis_index("expert")
+    me = lax.axis_index("tensor")
+    load = pltpu.make_async_copy(down_ref, down, load_sem.at[0])
+    load.start()
+    others = [lax.rem(me + n, 4) for n in (2, 1, 3)]
+    barrier = pltpu.get_barrier_semaphore()
+    for y in others:
+        pl.semaphore_signal(barrier, inc=1, device_id=(index, y), device_id_type=MESH)
+    dropped[me] = slice_ref[...]
+    pl.semaphore_wait(barrier, 3)
+    copies = [
+        pltpu.make_async_remote_copy(
+            src_ref=slice_ref, dst_ref=dropped.at[me], send_sem=send_sem.at[n], recv_sem=recv_sem.at[n],
+            device_id=(index, y), device_id_type=MESH,
+        )
+        for n, y in enumerate(others)
     ]
-    for copy in loads:
+    for copy in copies:
         copy.start()
     parts, rows, own = every_ref.shape
     count = chosen_ref.shape[1]
@@ -90,20 +104,19 @@
     rest = (removed - three(gh, gl, wh, wl)).astype(BF16)
     w = (w + dot(xh, rest)) * inverse_bound
     wh, wl = split(w)
-    me = lax.axis_index("tensor")
     mine = every_ref[me]
     units = lax.broadcasted_iota(jnp.int32, (own, count), 0) + me * own
     keep = 1.0 - jnp.sum((units == chosen).astype(F32), axis=1, keepdims=True)
     mixing = (dot(mine, wh, 0, 0) + dot(mine, wl, 0, 0)) * keep
     high, low = split(mixing)
-    for copy in loads:
+    load.wait()
+    for copy in copies:
         copy.wait()
-    width = down_ref.shape[1]
-    tile = width // TILES
+    tile = dropped.shape[2]
     stores = []
-    for n in range(TILES):
+    for n in range(4):
         at = slice(n * tile, (n + 1) * tile)
-        part = dropped[:, at]
+        part = dropped[n]
         change = dot(high, part) + dot(low, part)
         result[:, at] = ((down[:, at].astype(F32) + change) * keep).astype(BF16)
         stores.append(pltpu.make_async_copy(result.at[:, at], out_ref.at[:, at], store_sem.at[n]))
@@ -112,7 +125,7 @@
         copy.wait()
 
 
-def solve(every, chosen, down, dropped):
+def solve(every, chosen, down, part):
     own, width = down.shape
     count = chosen.shape[1]
     whole = pl.BlockSpec(memory_space=pltpu.VMEM)
@@ -120,31 +133,35 @@
     return pl.pallas_call(
         solve_kernel,
         out_shape=jax.ShapeDtypeStruct((own, width), BF16),
-        in_specs=[whole, whole, left, left],
+        in_specs=[whole, whole, left, whole],
         out_specs=left,
         scratch_shapes=[
             pltpu.VMEM((own, width), BF16),
-            pltpu.VMEM((count, width), BF16),
+            pltpu.VMEM((4, count, width // 4), BF16),
             pltpu.VMEM((own, width), BF16),
-            pltpu.SemaphoreType.DMA((2,)),
-            pltpu.SemaphoreType.DMA((TILES,)),
+            pltpu.SemaphoreType.DMA((1,)),
+            pltpu.SemaphoreType.DMA((4,)),
+            pltpu.SemaphoreType.DMA((3,)),
+            pltpu.SemaphoreType.DMA((3,)),
         ],
-        compiler_params=pltpu.CompilerParams(vmem_limit_bytes=48 * 2**20),
-    )(every, chosen, down, dropped)
+        compiler_params=pltpu.CompilerParams(
+            collective_id=1, has_side_effects=True, vmem_limit_bytes=48 * 2**20
+        ),
+    )(every, chosen, down, part)
 
 
 ZS, XS = 8, 4
 CHIPS = ZS * XS
 CORES = 2
 MOST = 8
-MESH = pl.DeviceIdType.MESH
 
 
 def dispatch_kernel(
-    tok_ref, route_ref, gate_ref, up_ref, every_ref,
+    tok_ref, route_ref, gate_ref, up_ref, down_ref, chosen_ref, every_ref, slice_ref,
     held, told, rows, other, gate_w, up_w, gate_sum, up_sum, hidden,
     held_send, held_recv, told_send, told_recv, rows_recv, sib_send, y_send, y_sib_send,
     pre_send, pre_recv, local_sem, weight_sem, hid_send, hid_recv,
+    down, term, gained, down_sem, drop_send, drop_recv,
 ):
     index = lax.axis_index("expert")
     t = lax.axis_index("tensor")
@@ -164,8 +181,8 @@
         pltpu.make_async_copy(gate_ref.at[0], gate_w, weight_sem.at[0]),
         pltpu.make_async_copy(up_ref.at[0], up_w, weight_sem.at[1]),
     ]
-    for load in loads:
-        load.start()
+    down_load = pltpu.make_async_copy(down_ref, down, down_sem.at[0])
+    down_load.start()
 
     barrier = pltpu.get_barrier_semaphore()
     partners = [(n, t) for n in (z_up, z_down, x_up, x_down)] + [(mate, t)]
@@ -205,7 +222,7 @@
             )
         )
     own.append(pltpu.make_async_copy(route_ref, told.at[here, core], local_sem.at[2]))
-    for copy in own:
+    for copy in own + loads:
         copy.start()
     for copy in own:
         copy.wait()
@@ -268,6 +285,20 @@
             go(c, here, to)
     pick([(0, here), (1, here)])
 
+    down_load.wait()
+    own_rows, count = down.shape[0], chosen_ref.shape[1]
+    units = lax.broadcasted_iota(jnp.int32, (own_rows, count), 0) + t * own_rows
+    picks = (units == chosen_ref[...]).astype(F32).astype(BF16)
+    share = term.shape[-1]
+    for u in range(4):
+        term[u] = dot(picks, down[:, u * share : (u + 1) * share], 0, 0).astype(BF16)
+    drops = [
+        remote(term.at[y], gained.at[n], drop_send.at[n], drop_recv.at[n], (index, y))
+        for n, y in enumerate((across, above, below))
+    ]
+    for copy in drops:
+        copy.start()
+
     def turn(r, carry):
         @pl.when(r <= 4)
         def _():
@@ -416,6 +447,12 @@
                 remote(mine, mine, hid_send.at[part, n], hid_recv.at[part, n], (index, y))
             )
             copies[-1].start()
+    for copy in drops:
+        copy.wait()
+    found = term[t].astype(F32)
+    for n in range(3):
+        found = found + gained[n].astype(F32)
+    slice_ref[...] = found.astype(BF16)
     gone = told.at[pl.ds(0, CHIPS - 1)]
     remote(gone, gone, told_send.at[0], told_recv.at[0], (mate, t)).wait_send()
     for c in range(2):
@@ -429,19 +466,24 @@
     every_ref[...] = hidden[...]
 
 
-def dispatch(tokens, told, gate_weight, up_weight):
+def dispatch(tokens, told, gate_weight, up_weight, down, chosen):
     tok_rows, width = tokens.shape
     own = gate_weight.shape[2]
     wide = width // 8
     slots = CHIPS * 2 * MOST
+    rows_own, width_out = down.shape
+    count, share = chosen.shape[1], width_out // 4
     whole = pl.BlockSpec(memory_space=pltpu.VMEM)
     left = pl.BlockSpec(memory_space=pl.ANY)
     dma = pltpu.SemaphoreType.DMA
     return pl.pallas_call(
         dispatch_kernel,
-        out_shape=jax.ShapeDtypeStruct((4, slots, own), BF16),
-        in_specs=[left, whole, left, left],
-        out_specs=whole,
+        out_shape=[
+            jax.ShapeDtypeStruct((4, slots, own), BF16),
+            jax.ShapeDtypeStruct((count, share), BF16),
+        ],
+        in_specs=[left, whole, left, left, left, whole],
+        out_specs=[whole, whole],
         scratch_shapes=[
             pltpu.VMEM((2, CHIPS, CORES * tok_rows, wide), BF16),
             pltpu.VMEM((CHIPS, CORES, 8, 128), jnp.int32),
@@ -454,6 +496,10 @@
             pltpu.VMEM((4, slots, own), BF16),
             dma((2,)), dma((2, CHIPS)), dma((1,)), dma((CHIPS,)), dma((8,)), dma((2,)), dma((2,)),
             dma((2,)), dma((3,)), dma((3,)), dma((3,)), dma((2,)), dma((2, 3)), dma((2, 3)),
+            pltpu.VMEM((rows_own, width_out), BF16),
+            pltpu.VMEM((4, count, share), BF16),
+            pltpu.VMEM((3, count, share), BF16),
+            dma((1,)), dma((3,)), dma((3,)),
         ],
         compiler_params=pltpu.CompilerParams(
             collective_id=0, has_side_effects=True, vmem_limit_bytes=48 * 2**20
@@ -461,25 +507,18 @@
         cost_estimate=pl.CostEstimate(
             flops=4 * slots * width * own, bytes_accessed=4 * width * own, transcendentals=slots * own
         ),
-    )(tokens, told, gate_weight, up_weight)
+    )(tokens, told, gate_weight, up_weight, down, chosen)
 
 
 def local(tokens, routes, gate_weight, up_weight, down_weight, removed):
-    me = lax.axis_index("tensor")
     tok_rows, top = routes.shape
     down = down_weight[0]
-    own_rows = down.shape[0]
-    chosen = removed
-    units = jnp.arange(own_rows, dtype=jnp.int32)[:, None] + me * own_rows
-    own_picks = (units == chosen).astype(BF16)
-    term = jnp.dot(own_picks.T, down, preferred_element_type=F32)
-    dropped = lax.psum(term.astype(BF16), "tensor")
     core = lax.rem(lax.axis_index("expert"), CORES)
     told = lax.dynamic_update_slice(
         jnp.full((top, 128), -1, jnp.int32), routes.T, (0, core * tok_rows)
     )
-    every = dispatch(tokens, told, gate_weight, up_weight)
-    return solve(every, chosen, down, dropped)[None]
+    every, part = dispatch(tokens, told, gate_weight, up_weight, down, removed)
+    return solve(every, removed, down, part)[None]
 
 
 def solution(mesh):

time: 141 us -> 118 us (0.84)
  between operations: 13.5 us -> 0.03 us
  Pallas kernels: 119 us -> 112 us
  matrix products: 3.5 us -> 0 us
    pallas_call x1, Pallas kernels: 101 us -> 86.8 us  [dispatch(): pl.pallas_call(dispatch_kernel, out_shape=[jax.ShapeDtypeStruct((4, slots...]
    pallas_call x1, Pallas kernels: 18.5 us -> 25.7 us  [solve(): pl.pallas_call(solve_kernel, out_shape=jax.ShapeDtypeStruct((own, width),...]
    dot_general x1 -> x0, matrix products: 3.5 us -> none  [local(): term = jnp.dot(own_picks.T, down, preferred_element_type=F32)]
    unnamed x12 -> x9, local copies, waits for them, and re-layouts: 4.36 us -> 4.43 us
  transfers between devices with their start and end apart: 1 -> 0, of which waited for: 0 -> 0; matrix products, arithmetic and copies ran while one was open for 0% -> 0% of each run, Pallas kernels for 71% -> 0%
where the time goes in v4:
time: 118 us
  Pallas kernels  112 us (95%)
  local copies, waits for them, and re-layouts  5.29 us (4%)
    pallas_call x1, Pallas kernels, dispatch(): pl.pallas_call(dispatch_kernel, out_shape=[jax.ShapeDtypeStruct((4, slots...  86.8 us
    pallas_call x1, Pallas kernels, solve(): pl.pallas_call(solve_kernel, out_shape=jax.ShapeDtypeStruct((own, width),...  25.7 us
    unnamed x9, local copies, waits for them, and re-layouts  4.43 us

profile of v4, /device:TPU:1, one launch (start us, length us, event | category | flops | bytes accessed | tf_op | source)
XLA Modules:
  0.0 117.8 jit_solution(13444934450436886216)
XLA Ops:
  0.0 0.9 dynamic_update_slice.3.route_ref
  0.9 0.0 copy-start
  0.9 1.5 %copy-done = bf16[1,256,3584]{2,1,0:T(8,128)(2,1)S(1)} copy-done((bf16[1,256,3584]{2,1,0:T(8,128)(2,1)S(1)}, bf16[1,256,3584]{2,1,0:T(8,128)(2,1)}, u32[]{:S(2)}) %copy-start) | copy-done | bytes 1835032
  2.4 0.0 copy-start.2
  2.4 0.7 copy-done.2
  3.0 0.0 copy-start.3
  3.0 1.0 copy-done.3
  4.1 0.0 copy-start.1
  4.1 86.8 %shard_map.64 = (bf16[4,512,256]{2,1,0:T(8,128)(2,1)S(1)}, bf16[256,896]{1,0:T(8,128)(2,1)S(1)}) custom-call(bf16[32,7168]{1,0:T(8,128)(2,1)S(1)} %copy-done.3, s32[8,128]{1,0:T(8,128)S(1)} %dynamic_update_slice.3.route_ref, bf16[1,7168,256]{2,1,0:T(8,128)(2,1)} %gate_ref.1, bf16[1,7168,256]{2,1,0:T(8,128)(2,1)} %up_ref.1, bf16[256,3584]{1,0:T(8,128)(2,1)S(1)} %bitcast.4, ...), custom_call_target="tpu_custom_call" | custom-call | flops 3758096384 | bytes 7340032 | tf_op jit(solution)/shard_map/pallas_call | solution.py:479
  90.9 0.0 copy-done.1
  90.9 25.7 %shard_map.65 = bf16[256,3584]{1,0:T(8,128)(2,1)S(1)} custom-call(bf16[4,512,256]{2,1,0:T(8,128)(2,1)S(1)} %get-tuple-element.7.every_ref, s32[1,256]{1,0:T(1,128)S(1)} %copy-done.2, bf16[256,3584]{1,0:T(8,128)(2,1)S(1)} %bitcast.5, bf16[256,896]{1,0:T(8,128)(2,1)S(1)} %get-tuple-element.8.slice_ref), custom_call_target="tpu_custom_call" | custom-call | tf_op jit(solution)/shard_map/pallas_call | solution.py:133
  116.6 1.2 %copy.9 = bf16[1,256,3584]{2,1,0:T(8,128)(2,1)} copy(bf16[1,256,3584]{2,1,0:T(8,128)(2,1)S(1)} %bitcast.3) | data formatting | bytes 3670016
  (1 shorter events, 0.0 us)
Async XLA Ops:
  0.9 1.5 %copy-start = (bf16[1,256,3584]{2,1,0:T(8,128)(2,1)S(1)}, bf16[1,256,3584]{2,1,0:T(8,128)(2,1)}, u32[]{:S(2)}) copy-start(bf16[1,256,3584]{2,1,0:T(8,128)(2,1)} %param.10) | copy-start | bytes 5505028
  2.4 0.7 copy-start.2
  3.0 1.0 copy-start.3
  4.1 86.8 %copy-start.1 = (bf16[1,256,3584]{2,1,0:T(8,128)(2,1)S(1)}, bf16[1,256,3584]{2,1,0:T(8,128)(2,1)}, u32[]{:S(2)}) copy-start(bf16[1,256,3584]{2,1,0:T(8,128)(2,1)} %param.10) | copy-start | bytes 5505028

commit v5 on v4

--- a/solution.py
+++ b/solution.py
@@ -44,7 +44,7 @@
     me = lax.axis_index("tensor")
     load = pltpu.make_async_copy(down_ref, down, load_sem.at[0])
     load.start()
-    others = [lax.rem(me + n, 4) for n in (2, 1, 3)]
+    others = [lax.rem(me + n, 4) for n in (1, 3, 2)]
     barrier = pltpu.get_barrier_semaphore()
     for y in others:
         pl.semaphore_signal(barrier, inc=1, device_id=(index, y), device_id_type=MESH)
@@ -110,13 +110,13 @@
     mixing = (dot(mine, wh, 0, 0) + dot(mine, wl, 0, 0)) * keep
     high, low = split(mixing)
     load.wait()
-    for copy in copies:
-        copy.wait()
     tile = dropped.shape[2]
     stores = []
-    for n in range(4):
-        at = slice(n * tile, (n + 1) * tile)
-        part = dropped[n]
+    for n, quarter in enumerate((me, others[1], others[0], others[2])):
+        if n:
+            copies[n - 1].wait()
+        at = pl.ds(pl.multiple_of(quarter * tile, 128), tile)
+        part = dropped[quarter]
         change = dot(high, part) + dot(low, part)
         result[:, at] = ((down[:, at].astype(F32) + change) * keep).astype(BF16)
         stores.append(pltpu.make_async_copy(result.at[:, at], out_ref.at[:, at], store_sem.at[n]))

time: 118 us -> 116 us (0.983)
    pallas_call x1, Pallas kernels: 25.7 us -> 23.7 us  [solve(): pl.pallas_call(solve_kernel, out_shape=jax.ShapeDtypeStruct((own, width),...]
where the time goes in v5:
time: 116 us
  Pallas kernels  111 us (96%)
  local copies, waits for them, and re-layouts  5.29 us (5%)
    pallas_call x1, Pallas kernels, dispatch(): pl.pallas_call(dispatch_kernel, out_shape=[jax.ShapeDtypeStruct((4, slots...  86.8 us
    pallas_call x1, Pallas kernels, solve(): pl.pallas_call(solve_kernel, out_shape=jax.ShapeDtypeStruct((own, width),...  23.7 us
    unnamed x9, local copies, waits for them, and re-layouts  4.43 us

profile of v5, /device:TPU:1, one launch (start us, length us, event | category | flops | bytes accessed | tf_op | source)
XLA Modules:
  0.0 115.9 jit_solution(17817153761127405886)
XLA Ops:
  0.0 0.9 dynamic_update_slice.3.route_ref
  0.9 0.0 copy-start
  0.9 1.5 %copy-done = bf16[1,256,3584]{2,1,0:T(8,128)(2,1)S(1)} copy-done((bf16[1,256,3584]{2,1,0:T(8,128)(2,1)S(1)}, bf16[1,256,3584]{2,1,0:T(8,128)(2,1)}, u32[]{:S(2)}) %copy-start) | copy-done | bytes 1835032
  2.4 0.0 copy-start.2
  2.4 0.7 copy-done.2
  3.0 0.0 copy-start.3
  3.0 1.0 copy-done.3
  4.1 0.0 copy-start.1
  4.1 86.8 %shard_map.64 = (bf16[4,512,256]{2,1,0:T(8,128)(2,1)S(1)}, bf16[256,896]{1,0:T(8,128)(2,1)S(1)}) custom-call(bf16[32,7168]{1,0:T(8,128)(2,1)S(1)} %copy-done.3, s32[8,128]{1,0:T(8,128)S(1)} %dynamic_update_slice.3.route_ref, bf16[1,7168,256]{2,1,0:T(8,128)(2,1)} %gate_ref.1, bf16[1,7168,256]{2,1,0:T(8,128)(2,1)} %up_ref.1, bf16[256,3584]{1,0:T(8,128)(2,1)S(1)} %bitcast.4, ...), custom_call_target="tpu_custom_call" | custom-call | flops 3758096384 | bytes 7340032 | tf_op jit(solution)/shard_map/pallas_call | solution.py:479
  90.9 0.0 copy-done.1
  90.9 23.7 %shard_map.65 = bf16[256,3584]{1,0:T(8,128)(2,1)S(1)} custom-call(bf16[4,512,256]{2,1,0:T(8,128)(2,1)S(1)} %get-tuple-element.7.every_ref, s32[1,256]{1,0:T(1,128)S(1)} %copy-done.2, bf16[256,3584]{1,0:T(8,128)(2,1)S(1)} %bitcast.5, bf16[256,896]{1,0:T(8,128)(2,1)S(1)} %get-tuple-element.8.slice_ref), custom_call_target="tpu_custom_call" | custom-call | tf_op jit(solution)/shard_map/pallas_call | solution.py:133
  114.6 1.2 %copy.9 = bf16[1,256,3584]{2,1,0:T(8,128)(2,1)} copy(bf16[1,256,3584]{2,1,0:T(8,128)(2,1)S(1)} %bitcast.3) | data formatting | bytes 3670016
  (1 shorter events, 0.0 us)
Async XLA Ops:
  0.9 1.5 %copy-start = (bf16[1,256,3584]{2,1,0:T(8,128)(2,1)S(1)}, bf16[1,256,3584]{2,1,0:T(8,128)(2,1)}, u32[]{:S(2)}) copy-start(bf16[1,256,3584]{2,1,0:T(8,128)(2,1)} %param.10) | copy-start | bytes 5505028
  2.4 0.7 copy-start.2
  3.0 1.0 copy-start.3
  4.1 86.8 %copy-start.1 = (bf16[1,256,3584]{2,1,0:T(8,128)(2,1)S(1)}, bf16[1,256,3584]{2,1,0:T(8,128)(2,1)}, u32[]{:S(2)}) copy-start(bf16[1,256,3584]{2,1,0:T(8,128)(2,1)} %param.10) | copy-start | bytes 5505028

commit v6 on v5

--- a/solution.py
+++ b/solution.py
@@ -224,6 +224,20 @@
     own.append(pltpu.make_async_copy(route_ref, told.at[here, core], local_sem.at[2]))
     for copy in own + loads:
         copy.start()
+    down_load.wait()
+    own_rows, count = down.shape[0], chosen_ref.shape[1]
+    units = lax.broadcasted_iota(jnp.int32, (own_rows, count), 0) + t * own_rows
+    picks = (units == chosen_ref[...]).astype(F32).astype(BF16)
+    share = term.shape[-1]
+    for u in range(4):
+        term[u] = dot(picks, down[:, u * share : (u + 1) * share], 0, 0).astype(BF16)
+    drops = [
+        remote(term.at[y], gained.at[n], drop_send.at[n], drop_recv.at[n], (index, y))
+        for n, y in enumerate((across, above, below))
+    ]
+    for copy in drops:
+        copy.start()
+
     for copy in own:
         copy.wait()
     for copy in first:
@@ -284,20 +298,6 @@
         for to in (z_up, z_down, x_up, x_down):
             go(c, here, to)
     pick([(0, here), (1, here)])
-
-    down_load.wait()
-    own_rows, count = down.shape[0], chosen_ref.shape[1]
-    units = lax.broadcasted_iota(jnp.int32, (own_rows, count), 0) + t * own_rows
-    picks = (units == chosen_ref[...]).astype(F32).astype(BF16)
-    share = term.shape[-1]
-    for u in range(4):
-        term[u] = dot(picks, down[:, u * share : (u + 1) * share], 0, 0).astype(BF16)
-    drops = [
-        remote(term.at[y], gained.at[n], drop_send.at[n], drop_recv.at[n], (index, y))
-        for n, y in enumerate((across, above, below))
-    ]
-    for copy in drops:
-        copy.start()
 
     def turn(r, carry):
         @pl.when(r <= 4)

time: 116 us -> 116 us (level)
  no operation moved by 1% of the time
where the time goes in v6:
time: 116 us; the launch traced here: 115 us
  Pallas kernels  110 us (95%)
  local copies, waits for them, and re-layouts  5.29 us (5%)
    pallas_call x1, Pallas kernels, dispatch(): pl.pallas_call(dispatch_kernel, out_shape=[jax.ShapeDtypeStruct((4, slots...  86.1 us
    pallas_call x1, Pallas kernels, solve(): pl.pallas_call(solve_kernel, out_shape=jax.ShapeDtypeStruct((own, width),...  24 us
    unnamed x9, local copies, waits for them, and re-layouts  4.43 us

profile of v6, /device:TPU:1, one launch (start us, length us, event | category | flops | bytes accessed | tf_op | source)
XLA Modules:
  0.0 115.4 jit_solution(1176229919950302631)
XLA Ops:
  0.0 0.9 dynamic_update_slice.3.route_ref
  0.9 0.0 copy-start
  0.9 1.5 %copy-done = bf16[1,256,3584]{2,1,0:T(8,128)(2,1)S(1)} copy-done((bf16[1,256,3584]{2,1,0:T(8,128)(2,1)S(1)}, bf16[1,256,3584]{2,1,0:T(8,128)(2,1)}, u32[]{:S(2)}) %copy-start) | copy-done | bytes 1835032
  2.4 0.0 copy-start.2
  2.4 0.7 copy-done.2
  3.0 0.0 copy-start.3
  3.0 1.0 copy-done.3
  4.1 0.0 copy-start.1
  4.1 86.1 %shard_map.64 = (bf16[4,512,256]{2,1,0:T(8,128)(2,1)S(1)}, bf16[256,896]{1,0:T(8,128)(2,1)S(1)}) custom-call(bf16[32,7168]{1,0:T(8,128)(2,1)S(1)} %copy-done.3, s32[8,128]{1,0:T(8,128)S(1)} %dynamic_update_slice.3.route_ref, bf16[1,7168,256]{2,1,0:T(8,128)(2,1)} %gate_ref.1, bf16[1,7168,256]{2,1,0:T(8,128)(2,1)} %up_ref.1, bf16[256,3584]{1,0:T(8,128)(2,1)S(1)} %bitcast.4, ...), custom_call_target="tpu_custom_call" | custom-call | flops 3758096384 | bytes 7340032 | tf_op jit(solution)/shard_map/pallas_call | solution.py:479
  90.2 0.0 copy-done.1
  90.2 24.0 %shard_map.65 = bf16[256,3584]{1,0:T(8,128)(2,1)S(1)} custom-call(bf16[4,512,256]{2,1,0:T(8,128)(2,1)S(1)} %get-tuple-element.7.every_ref, s32[1,256]{1,0:T(1,128)S(1)} %copy-done.2, bf16[256,3584]{1,0:T(8,128)(2,1)S(1)} %bitcast.5, bf16[256,896]{1,0:T(8,128)(2,1)S(1)} %get-tuple-element.8.slice_ref), custom_call_target="tpu_custom_call" | custom-call | tf_op jit(solution)/shard_map/pallas_call | solution.py:133
  114.2 1.2 %copy.9 = bf16[1,256,3584]{2,1,0:T(8,128)(2,1)} copy(bf16[1,256,3584]{2,1,0:T(8,128)(2,1)S(1)} %bitcast.3) | data formatting | bytes 3670016
  (1 shorter events, 0.0 us)
Async XLA Ops:
  0.9 1.5 %copy-start = (bf16[1,256,3584]{2,1,0:T(8,128)(2,1)S(1)}, bf16[1,256,3584]{2,1,0:T(8,128)(2,1)}, u32[]{:S(2)}) copy-start(bf16[1,256,3584]{2,1,0:T(8,128)(2,1)} %param.10) | copy-start | bytes 5505028
  2.4 0.7 copy-start.2
  3.0 1.0 copy-start.3
  4.1 86.2 %copy-start.1 = (bf16[1,256,3584]{2,1,0:T(8,128)(2,1)S(1)}, bf16[1,256,3584]{2,1,0:T(8,128)(2,1)}, u32[]{:S(2)}) copy-start(bf16[1,256,3584]{2,1,0:T(8,128)(2,1)} %param.10) | copy-start | bytes 5505028
